TPU v7x, 32 devices: a whole 2x2x4 slice. The times are simulated.
32 devices in a mesh: page: 4 (over y, x), strip: 8 (over z, core).
Axes of the slice: x: 2, y: 2, z: 4, core: 2. Of those that a mesh axis runs over, the one named last changes fastest.
Arguments:
- vis_tokens: bfloat16 [4, 96, 84, 768], P('page', 'strip'), may hold values from -6 to 6
- query_tokens: bfloat16 [4, 256, 768], P('page', 'strip'), may hold values from -6 to 6
- region_ids: int32 [4, 96, 84], P('page'), may hold values from 0 to 2
- query_mask: int32 [4, 256], P('page'), may hold values 0 or 1
- answer_len: int32 [4], P('page'), may hold values from 32 to 160, as said below
- norm1_gain: float32 [2, 768], replicated, may hold values from 0.5 to 1.5
- norm1_bias: float32 [2, 768], replicated, may hold values from -1.25 to 1.25
- qkv_weight: bfloat16 [2, 768, 2304], replicated, may hold values from -0.21875 to 0.21875
- out_weight: bfloat16 [2, 768, 768], replicated, may hold values from -4 to 4
- out_bias: float32 [2, 768], replicated, may hold values from -1.25 to 1.25
- norm2_gain: float32 [2, 768], replicated, may hold values from 0.5 to 1.5
- norm2_bias: float32 [2, 768], replicated, may hold values from -1.25 to 1.25
- up_weight: bfloat16 [2, 768, 3072], replicated, may hold values from -0.21875 to 0.21875
- up_bias: float32 [2, 3072], replicated, may hold values from -1.25 to 1.25
- down_weight: bfloat16 [2, 3072, 768], replicated, may hold values from -0.109375 to 0.109375
- down_bias: float32 [2, 768], replicated, may hold values from -1.25 to 1.25
- vis_cotangent: bfloat16 [4, 96, 84, 768], P('page', 'strip'), may hold values from -6 to 6
- query_cotangent: bfloat16 [4, 256, 768], P('page', 'strip'), may hold values from -6 to 6
Outputs:
- vis_out: bfloat16 [4, 96, 84, 768], P('page', 'strip')
- query_out: bfloat16 [4, 256, 768], P('page', 'strip')
- vis_grad: bfloat16 [4, 96, 84, 768], P('page', 'strip')
- query_grad: bfloat16 [4, 256, 768], P('page', 'strip')
- grad_norm1_gain: float32 [2, 768], P(None, 'strip')
- grad_norm1_bias: float32 [2, 768], P(None, 'strip')
- grad_qkv_weight: float32 [2, 768, 2304], P(None, 'strip')
- grad_out_weight: float32 [2, 768, 768], P(None, 'strip')
- grad_out_bias: float32 [2, 768], P(None, 'strip')
- grad_norm2_gain: float32 [2, 768], P(None, 'strip')
- grad_norm2_bias: float32 [2, 768], P(None, 'strip')
- grad_up_weight: float32 [2, 768, 3072], P(None, 'strip')
- grad_up_bias: float32 [2, 3072], P(None, 'strip')
- grad_down_weight: float32 [2, 3072, 768], P(None, 'strip')
- grad_down_bias: float32 [2, 768], P(None, 'strip')
Inputs may be any that keep to these rules, and one draw needn't show every extreme that they name: Some page's answer_len is exactly 160.
All inputs are finite; a program needn't handle non-finite values. No bound on the sum of `query_mask` on one device may be relied on, other than what follows from the above.
Results may differ from a plain program's by a relative error of at most 0.014.
Values may be sent and summed in bfloat16 or wider, within the bound.
No kernel may reach another device: no remote copies, remote signals or barrier semaphores. Data moves between devices by JAX's collectives and lax.ppermute only.
A program may use at most 448 MiB of HBM per device.

v0:
```python
import jax
import jax.numpy as jnp
from jax import lax
from jax.sharding import PartitionSpec as P

HEADS = 12
WIN = 12
SHIFT = 6


masked_value = -1000000000.0


def shifted(block, axis, distance):
    devices = range(lax.axis_size(axis))
    route = [((i - distance) % len(devices), i) for i in devices]
    return lax.ppermute(block, axis, route)


def layer_norm(values, gain, bias):
    center = values - jnp.mean(values, -1, keepdims=True)
    spread = jnp.mean(center * center, -1, keepdims=True)
    return center * lax.rsqrt(spread + 1e-05) * gain + bias


def inner(operand_a, operand_b):
    return lax.dot_general(
        operand_a, operand_b, (((0,), (0,)), ((), ())), preferred_element_type=jnp.float32
    )


def times_t(operand_a, operand_b):
    return lax.dot_general(
        operand_a, operand_b, (((1,), (1,)), ((), ())), preferred_element_type=jnp.float32
    )


def matmul(operand_a, operand_b):
    return jnp.dot(operand_a, operand_b, preferred_element_type=jnp.float32)


def gelu_exact(values):
    return jax.nn.gelu(values, approximate=False)


def to_windows(row_block):
    features = row_block.shape[-1]
    across = row_block.shape[1] // WIN
    return (
        row_block.reshape(WIN, across, WIN, features)
        .transpose(1, 0, 2, 3)
        .reshape(across, WIN * WIN, features)
    )


def from_windows(windows):
    across = windows.shape[0]
    features = windows.shape[-1]
    return (
        windows.reshape(across, WIN, WIN, features)
        .transpose(1, 0, 2, 3)
        .reshape(WIN, across * WIN, features)
    )


def body(
    vis_tokens,
    query_tokens,
    region_ids,
    query_mask,
    answer_len,
    norm1_gain,
    norm1_bias,
    qkv_weight,
    out_weight,
    out_bias,
    norm2_gain,
    norm2_bias,
    up_weight,
    up_bias,
    down_weight,
    down_bias,
    vis_cotangent,
    query_cotangent,
):
    strip_index = lax.axis_index("strip")
    local_rows, columns, features = vis_tokens.shape[1:]
    own_count = query_tokens.shape[1]
    head_count = HEADS
    head_size = features // head_count
    score_scale = head_size ** (-0.5)
    region = region_ids[0]
    total_rows = region.shape[0]
    key_open = query_mask[0] > 0
    query_count = key_open.shape[0]
    answer_size = answer_len[0]
    key_ids = jnp.arange(query_count, dtype=jnp.int32)
    prompt_open = key_open & (key_ids < query_count - answer_size)
    block_count = local_rows // WIN
    across = columns // WIN
    window_cells = WIN * WIN
    cell_count = local_rows * columns
    own_start = strip_index * own_count
    head_rows, head_cot = shifted((vis_tokens[0][:SHIFT], vis_cotangent[0][:SHIFT]), "strip", -1)
    vis_rows = jnp.concatenate([vis_tokens[0][SHIFT:], head_rows], 0)
    cot_rows = jnp.concatenate([vis_cotangent[0][SHIFT:], head_cot], 0)
    vis = vis_rows.astype(jnp.float32).reshape(cell_count, features)
    query = query_tokens[0].astype(jnp.float32)
    vis_norm = layer_norm(vis, norm1_gain[0], norm1_bias[0]).astype(jnp.bfloat16)
    query_norm = layer_norm(query, norm1_gain[1], norm1_bias[1]).astype(jnp.bfloat16)
    vis_qkv = matmul(vis_norm, qkv_weight[0]).astype(jnp.bfloat16)
    query_qkv = matmul(query_norm, qkv_weight[1]).astype(jnp.bfloat16)
    all_qkv = lax.all_gather(query_qkv, "strip", axis=0, tiled=True)
    all_q = all_qkv[:, :features].reshape(query_count, head_count, head_size)
    all_k = all_qkv[:, features : 2 * features].reshape(query_count, head_count, head_size)
    all_v = all_qkv[:, 2 * features :].reshape(query_count, head_count, head_size)
    row_ids = (
        strip_index * local_rows + SHIFT + jnp.arange(local_rows, dtype=jnp.int32)
    ) % total_rows
    rows_region = jnp.take(region, row_ids, axis=0)

    def to_blocks(values):
        rolled = jnp.roll(values, -SHIFT, axis=1)
        return rolled.reshape((block_count, WIN) + rolled.shape[1:])

    def from_blocks(values):
        joined = values.reshape((local_rows,) + values.shape[2:])
        return jnp.roll(joined, SHIFT, axis=1)

    q_blocks = to_blocks(vis_qkv[:, :features].reshape(local_rows, columns, features))
    kv_blocks = to_blocks(vis_qkv[:, features:].reshape(local_rows, columns, 2 * features))
    region_blocks = to_blocks(rows_region)

    def split_windows(q_block, kv_block, region_block):
        q_win = to_windows(q_block).reshape(across, window_cells, head_count, head_size)
        k_win = to_windows(kv_block[..., :features]).reshape(
            across, window_cells, head_count, head_size
        )
        v_win = to_windows(kv_block[..., features:]).reshape(
            across, window_cells, head_count, head_size
        )
        region_win = to_windows(region_block[..., None])[..., 0]
        return (q_win, k_win, v_win, region_win)

    def window_scores(q_win, k_win, region_win):
        local_scores = score_scale * jnp.einsum(
            "wqhd,wkhd->whqk", q_win, k_win, preferred_element_type=jnp.float32
        )
        same_region = region_win[:, None, :, None] == region_win[:, None, None, :]
        local_scores = jnp.where(same_region, local_scores, masked_value)
        cross_scores = score_scale * jnp.einsum(
            "wqhd,khd->whqk", q_win, all_k, preferred_element_type=jnp.float32
        )
        cross_scores = jnp.where(prompt_open[None, None, None, :], cross_scores, masked_value)
        return (local_scores, cross_scores)

    def window_forward(inputs):
        q_win, k_win, v_win, region_win = split_windows(inputs[0], inputs[1], inputs[2])
        local_scores, cross_scores = window_scores(q_win, k_win, region_win)
        row_top = jnp.maximum(local_scores.max(-1), cross_scores.max(-1))
        local_exp = jnp.exp(local_scores - row_top[..., None])
        cross_exp = jnp.exp(cross_scores - row_top[..., None])
        row_total = local_exp.sum(-1) + cross_exp.sum(-1)
        mixture = jnp.einsum(
            "whqk,wkhd->wqhd", local_exp, v_win, preferred_element_type=jnp.float32
        )
        mixture = mixture + jnp.einsum(
            "whqk,khd->wqhd", cross_exp, all_v, preferred_element_type=jnp.float32
        )
        mixture = mixture / jnp.swapaxes(row_total, 1, 2)[..., None]
        log_total = jnp.swapaxes(row_top + jnp.log(row_total), 1, 2)
        return (
            from_windows(mixture.reshape(across, window_cells, features)),
            from_windows(log_total),
        )

    win_out, win_lse = lax.map(window_forward, (q_blocks, kv_blocks, region_blocks))
    vis_attn = from_blocks(win_out).reshape(cell_count, features)
    vis_k = vis_qkv[:, features : 2 * features].reshape(cell_count, head_count, head_size)
    vis_v = vis_qkv[:, 2 * features :].reshape(cell_count, head_count, head_size)

    def seen_scores():
        return score_scale * jnp.einsum(
            "qhd,khd->hqk", all_q, vis_k, preferred_element_type=jnp.float32
        )

    vis_scores = seen_scores()
    full_top = lax.pmax(jnp.swapaxes(vis_scores.max(-1), 0, 1), "strip")
    weights_exp = jnp.exp(vis_scores - jnp.swapaxes(full_top, 0, 1)[..., None])
    part_total = jnp.swapaxes(weights_exp.sum(-1), 0, 1)
    part_mix = jnp.einsum(
        "hqk,khd->qhd", weights_exp, vis_v, preferred_element_type=jnp.float32
    ).reshape(query_count, features)
    part_total, part_mix = (part_total, part_mix)
    own_mix, own_total = (
        lax.psum_scatter(part_mix, "strip", scatter_dimension=0, tiled=True),
        lax.psum_scatter(part_total, "strip", scatter_dimension=0, tiled=True),
    )
    own_top = lax.dynamic_slice_in_dim(full_top, own_start, own_count, 0)
    own_q = query_qkv[:, :features].reshape(own_count, head_count, head_size)
    positions = own_start + jnp.arange(own_count, dtype=jnp.int32)
    self_open = key_open[None, :] & (
        (key_ids[None, :] < query_count - answer_size) | (key_ids[None, :] <= positions[:, None])
    )
    self_scores = score_scale * jnp.einsum(
        "qhd,khd->hqk", own_q, all_k, preferred_element_type=jnp.float32
    )
    self_scores = jnp.where(self_open[None], self_scores, masked_value)
    own_top_h = jnp.swapaxes(own_top, 0, 1)
    row_top = jnp.maximum(own_top_h, self_scores.max(-1))
    self_exp = jnp.exp(self_scores - row_top[..., None])
    carried = jnp.exp(own_top_h - row_top)
    row_total = jnp.swapaxes(own_total, 0, 1) * carried + self_exp.sum(-1)
    mixture = (
        own_mix.reshape(own_count, head_count, head_size) * jnp.swapaxes(carried, 0, 1)[..., None]
    )
    mixture = mixture + jnp.einsum(
        "hqk,khd->qhd", self_exp, all_v, preferred_element_type=jnp.float32
    )
    query_attn = (mixture / jnp.swapaxes(row_total, 0, 1)[..., None]).reshape(own_count, features)
    query_lse = jnp.swapaxes(row_top + jnp.log(row_total), 0, 1)

    def finish(values, attended, stream):
        attended_low = attended.astype(jnp.bfloat16)
        after_attn = values + matmul(attended_low, out_weight[stream]) + out_bias[stream]
        hidden_in = layer_norm(after_attn, norm2_gain[stream], norm2_bias[stream]).astype(
            jnp.bfloat16
        )
        pre_gelu = matmul(hidden_in, up_weight[stream]) + up_bias[stream]
        hidden = gelu_exact(pre_gelu).astype(jnp.bfloat16)
        result = after_attn + matmul(hidden, down_weight[stream]) + down_bias[stream]
        return (
            result.astype(jnp.bfloat16),
            (attended_low, after_attn, hidden_in, pre_gelu, hidden),
        )

    def finish_back(kept, cotangent, stream):
        attended_low, after_attn, hidden_in, pre_gelu, hidden = kept
        outer = cotangent.astype(jnp.float32)
        down_grad = inner(hidden, cotangent)
        down_bias_grad = jnp.sum(outer, 0)
        _, gelu_pull = jax.vjp(gelu_exact, pre_gelu)
        pre_grad = gelu_pull(times_t(cotangent, down_weight[stream]))[0].astype(jnp.bfloat16)
        up_grad = inner(hidden_in, pre_grad)
        up_bias_grad = jnp.sum(pre_grad.astype(jnp.float32), 0)
        _, norm_pull = jax.vjp(layer_norm, after_attn, norm2_gain[stream], norm2_bias[stream])
        after_grad, gain_grad, bias_grad = norm_pull(times_t(pre_grad, up_weight[stream]))
        after_grad = after_grad + outer
        branch_grad = after_grad.astype(jnp.bfloat16)
        out_grad = inner(attended_low, branch_grad)
        out_bias_grad = jnp.sum(branch_grad.astype(jnp.float32), 0)
        attended_grad = times_t(branch_grad, out_weight[stream]).astype(jnp.bfloat16)
        return (
            after_grad,
            attended_grad,
            (
                gain_grad,
                bias_grad,
                out_grad,
                out_bias_grad,
                up_grad,
                up_bias_grad,
                down_grad,
                down_bias_grad,
            ),
        )

    def start_back(values, normed, qkv_grad, after_grad, stream):
        weight_grad = inner(normed, qkv_grad)
        _, norm_pull = jax.vjp(layer_norm, values, norm1_gain[stream], norm1_bias[stream])
        input_grad, gain_grad, bias_grad = norm_pull(times_t(qkv_grad, qkv_weight[stream]))
        return ((input_grad + after_grad).astype(jnp.bfloat16), (gain_grad, bias_grad, weight_grad))

    vis_result, vis_kept = finish(vis, vis_attn, 0)
    query_result, query_kept = finish(query, query_attn, 1)
    vis_after, vis_dattn, vis_tail = finish_back(
        vis_kept, cot_rows.reshape(cell_count, features), 0
    )
    query_after, query_dattn, query_tail = finish_back(query_kept, query_cotangent[0], 1)
    vis_delta = (
        (vis_dattn.astype(jnp.float32) * vis_attn)
        .reshape(cell_count, head_count, head_size)
        .sum(-1)
    )
    grad_blocks = to_blocks(vis_dattn.reshape(local_rows, columns, features))
    delta_blocks = to_blocks(vis_delta.reshape(local_rows, columns, head_count))

    def window_backward(carried_sums, inputs):
        q_block, kv_block, region_block, grad_block, lse_block, delta_block = inputs
        q_win, k_win, v_win, region_win = split_windows(q_block, kv_block, region_block)
        grad_win = to_windows(grad_block).reshape(across, window_cells, head_count, head_size)
        lse_win = jnp.swapaxes(to_windows(lse_block), 1, 2)[..., None]
        delta_win = jnp.swapaxes(to_windows(delta_block), 1, 2)[..., None]
        local_scores, cross_scores = window_scores(q_win, k_win, region_win)
        local_prob = jnp.exp(local_scores - lse_win)
        cross_prob = jnp.exp(cross_scores - lse_win)
        local_dp = jnp.einsum(
            "wqhd,wkhd->whqk", grad_win, v_win, preferred_element_type=jnp.float32
        )
        cross_dp = jnp.einsum("wqhd,khd->whqk", grad_win, all_v, preferred_element_type=jnp.float32)
        local_ds = (local_prob * (local_dp - delta_win)).astype(jnp.bfloat16)
        cross_ds = (cross_prob * (cross_dp - delta_win)).astype(jnp.bfloat16)
        grad_q = jnp.einsum("whqk,wkhd->wqhd", local_ds, k_win, preferred_element_type=jnp.float32)
        grad_q = score_scale * (
            grad_q
            + jnp.einsum("whqk,khd->wqhd", cross_ds, all_k, preferred_element_type=jnp.float32)
        )
        grad_k = score_scale * jnp.einsum(
            "whqk,wqhd->wkhd", local_ds, q_win, preferred_element_type=jnp.float32
        )
        grad_v = jnp.einsum(
            "whqk,wqhd->wkhd", local_prob, grad_win, preferred_element_type=jnp.float32
        )
        key_grad = score_scale * jnp.einsum(
            "whqk,wqhd->khd", cross_ds, q_win, preferred_element_type=jnp.float32
        )
        value_grad = jnp.einsum(
            "whqk,wqhd->khd", cross_prob, grad_win, preferred_element_type=jnp.float32
        )
        grad_kv = jnp.concatenate(
            [
                grad_k.reshape(across, window_cells, features),
                grad_v.reshape(across, window_cells, features),
            ],
            -1,
        )
        sums = (
            carried_sums[0] + key_grad.reshape(query_count, features),
            carried_sums[1] + value_grad.reshape(query_count, features),
        )
        return (
            sums,
            (from_windows(grad_q.reshape(across, window_cells, features)), from_windows(grad_kv)),
        )

    zero_rows = jnp.zeros((query_count, features), jnp.float32)
    window_sums, (win_grad_q, win_grad_kv) = lax.scan(
        window_backward,
        (zero_rows, zero_rows),
        (q_blocks, kv_blocks, region_blocks, grad_blocks, win_lse, delta_blocks),
    )
    vis_grad_q = from_blocks(win_grad_q).reshape(cell_count, features)
    local_grad_kv = from_blocks(win_grad_kv).reshape(cell_count, 2 * features)
    query_delta = (
        (query_dattn.astype(jnp.float32) * query_attn)
        .reshape(own_count, head_count, head_size)
        .sum(-1)
    )
    all_grad = lax.all_gather(query_dattn, "strip", axis=0, tiled=True)
    all_lse, all_delta = (
        lax.all_gather(query_lse, "strip", axis=0, tiled=True),
        lax.all_gather(query_delta, "strip", axis=0, tiled=True),
    )
    grad_heads = all_grad.reshape(query_count, head_count, head_size)
    vis_prob = jnp.exp(seen_scores() - jnp.swapaxes(all_lse, 0, 1)[..., None])
    vis_dp = jnp.einsum("qhd,khd->hqk", grad_heads, vis_v, preferred_element_type=jnp.float32)
    vis_ds = (vis_prob * (vis_dp - jnp.swapaxes(all_delta, 0, 1)[..., None])).astype(jnp.bfloat16)
    far_q = score_scale * jnp.einsum(
        "hqk,khd->qhd", vis_ds, vis_k, preferred_element_type=jnp.float32
    ).reshape(query_count, features)
    near_k = score_scale * jnp.einsum(
        "hqk,qhd->khd", vis_ds, all_q, preferred_element_type=jnp.float32
    ).reshape(cell_count, features)
    near_v = jnp.einsum(
        "hqk,qhd->khd", vis_prob, grad_heads, preferred_element_type=jnp.float32
    ).reshape(cell_count, features)
    own_grad = query_dattn.reshape(own_count, head_count, head_size)
    self_prob = jnp.exp(self_scores - jnp.swapaxes(query_lse, 0, 1)[..., None])
    self_dp = jnp.einsum("qhd,khd->hqk", own_grad, all_v, preferred_element_type=jnp.float32)
    self_ds = (self_prob * (self_dp - jnp.swapaxes(query_delta, 0, 1)[..., None])).astype(
        jnp.bfloat16
    )
    self_q = score_scale * jnp.einsum(
        "hqk,khd->qhd", self_ds, all_k, preferred_element_type=jnp.float32
    ).reshape(own_count, features)
    key_part = window_sums[0] + score_scale * jnp.einsum(
        "hqk,qhd->khd", self_ds, own_q, preferred_element_type=jnp.float32
    ).reshape(query_count, features)
    value_part = window_sums[1] + jnp.einsum(
        "hqk,qhd->khd", self_prob, own_grad, preferred_element_type=jnp.float32
    ).reshape(query_count, features)
    sum_q, sum_k, sum_v = (
        lax.psum_scatter(far_q, "strip", scatter_dimension=0, tiled=True),
        lax.psum_scatter(key_part, "strip", scatter_dimension=0, tiled=True),
        lax.psum_scatter(value_part, "strip", scatter_dimension=0, tiled=True),
    )
    query_dqkv = jnp.concatenate([self_q + sum_q, sum_k, sum_v], -1).astype(jnp.bfloat16)
    own_kv = local_grad_kv + jnp.concatenate([near_k, near_v], -1)
    vis_dqkv = jnp.concatenate([vis_grad_q, own_kv], -1).astype(jnp.bfloat16)
    vis_input_grad, vis_head = start_back(vis, vis_norm, vis_dqkv, vis_after, 0)
    query_input_grad, query_head = start_back(query, query_norm, query_dqkv, query_after, 1)
    vis_grid = vis_result.reshape(local_rows, columns, features)
    grad_grid = vis_input_grad.reshape(local_rows, columns, features)
    tail_out, tail_grad = shifted(
        (vis_grid[local_rows - SHIFT :], grad_grid[local_rows - SHIFT :]), "strip", 1
    )
    vis_final = jnp.concatenate([tail_out, vis_grid[: local_rows - SHIFT]], 0)
    grad_final = jnp.concatenate([tail_grad, grad_grid[: local_rows - SHIFT]], 0)
    gain_one = jnp.stack([vis_head[0], query_head[0]])
    bias_one = jnp.stack([vis_head[1], query_head[1]])
    qkv_grad = jnp.stack([vis_head[2], query_head[2]])
    gain_two = jnp.stack([vis_tail[0], query_tail[0]])
    bias_two = jnp.stack([vis_tail[1], query_tail[1]])
    out_grad = jnp.stack([vis_tail[2], query_tail[2]])
    obias_grad = jnp.stack([vis_tail[3], query_tail[3]])
    up_grad = jnp.stack([vis_tail[4], query_tail[4]])
    ubias_grad = jnp.stack([vis_tail[5], query_tail[5]])
    down_grad = jnp.stack([vis_tail[6], query_tail[6]])
    dbias_grad = jnp.stack([vis_tail[7], query_tail[7]])
    (
        gain_one,
        bias_one,
        qkv_grad,
        out_grad,
        obias_grad,
        gain_two,
        bias_two,
        up_grad,
        ubias_grad,
        down_grad,
        dbias_grad,
    ) = (
        lax.psum_scatter(gain_one, "strip", scatter_dimension=1, tiled=True),
        lax.psum_scatter(bias_one, "strip", scatter_dimension=1, tiled=True),
        lax.psum_scatter(qkv_grad, "strip", scatter_dimension=1, tiled=True),
        lax.psum_scatter(out_grad, "strip", scatter_dimension=1, tiled=True),
        lax.psum_scatter(obias_grad, "strip", scatter_dimension=1, tiled=True),
        lax.psum_scatter(gain_two, "strip", scatter_dimension=1, tiled=True),
        lax.psum_scatter(bias_two, "strip", scatter_dimension=1, tiled=True),
        lax.psum_scatter(up_grad, "strip", scatter_dimension=1, tiled=True),
        lax.psum_scatter(ubias_grad, "strip", scatter_dimension=1, tiled=True),
        lax.psum_scatter(down_grad, "strip", scatter_dimension=1, tiled=True),
        lax.psum_scatter(dbias_grad, "strip", scatter_dimension=1, tiled=True),
    )
    (
        gain_one,
        bias_one,
        qkv_grad,
        out_grad,
        obias_grad,
        gain_two,
        bias_two,
        up_grad,
        ubias_grad,
        down_grad,
        dbias_grad,
    ) = lax.psum(
        (
            gain_one,
            bias_one,
            qkv_grad,
            out_grad,
            obias_grad,
            gain_two,
            bias_two,
            up_grad,
            ubias_grad,
            down_grad,
            dbias_grad,
        ),
        "page",
    )
    return (
        vis_final.reshape(1, local_rows, columns, features),
        query_result.reshape(1, own_count, features),
        grad_final.reshape(1, local_rows, columns, features),
        query_input_grad.reshape(1, own_count, features),
        gain_one,
        bias_one,
        qkv_grad,
        out_grad,
        obias_grad,
        gain_two,
        bias_two,
        up_grad,
        ubias_grad,
        down_grad,
        dbias_grad,
    )


def solution(mesh):
    return jax.shard_map(
        body,
        mesh=mesh,
        in_specs=(
            P("page", "strip", None, None),
            P("page", "strip", None),
            P("page", None, None),
            P("page", None),
            P("page"),
            P(),
            P(),
            P(),
            P(),
            P(),
            P(),
            P(),
            P(),
            P(),
            P(),
            P(),
            P("page", "strip", None, None),
            P("page", "strip", None),
        ),
        out_specs=(
            P("page", "strip", None, None),
            P("page", "strip", None),
            P("page", "strip", None, None),
            P("page", "strip", None),
            P(None, "strip"),
            P(None, "strip"),
            P(None, "strip", None),
            P(None, "strip", None),
            P(None, "strip"),
            P(None, "strip"),
            P(None, "strip"),
            P(None, "strip", None),
            P(None, "strip"),
            P(None, "strip", None),
            P(None, "strip"),
        ),
        check_vma=False,
    )
```

profile of v0, /device:TPU:0, one launch (start us, length us, event | category | flops | bytes accessed | tf_op | source)
XLA Modules:
  0.0 1655.6 jit_solution(6221050989781145063)
XLA Ops:
  146.1 10.2 fusion.22
  173.0 8.5 fusion.223
  194.2 9.6 copy.274
  229.5 36.3 %multiply_convert_fusion.2 = (bf16[1008,3072]{1,0:T(8,128)(2,1)}, f32[1008,3072]{1,0:T(8,128)}, f32[1008,3072]{1,0:T(8,128)}) fusion(f32[3072]{0:T(1024)S(1)} %bitcast.468, bf16[2,768,3072]{2,1,0:T(8,128)(2,1)} %param.30, f32[1008,768]{1,0:T(8,128)S(1)} %get-tuple-element.165, f32[768]{0:T(1024)S(1)} %get-tuple-element.100, ...), kind=kOutput, calls=%fused_computation.23 | convolution fusion | flops 4964585472 | bytes 38807424 | tf_op jit(solution)/shard_map/dot_general | solution.py:39
  265.8 17.4 %convert_reduce_fusion = (f32[3072]{0:T(1024)}, bf16[1008,3072]{1,0:T(8,128)(2,1)}) fusion(f32[1008,3072]{1,0:T(8,128)} %get-tuple-element.134, bf16[1008,768]{1,0:T(8,128)(2,1)S(1)} %copy-done.15, bf16[2,3072,768]{2,1,0:T(8,128)(2,1)} %param.32, f32[1008,3072]{1,0:T(8,128)} %get-tuple-element.166, f32[3072]{0:T(1024)S(1)} %bitcast.469), kind=kOutput, calls=%fused_computation.16 | convolution fusion | flops 4808979456 | bytes 37257216 | tf_op jit(solution)/shard_map/dot_general | solution.py:33
  283.1 10.0 multiply_reduce_fusion.2
  314.3 25.9 %pmax.7 = f32[256,12]{0,1:T(8,128)S(1)} all-reduce(f32[256,12]{0,1:T(8,128)S(1)} %bitcast.458), channel_id=1, replica_groups=mesh['page'=4,'strip'=8] {'strip'}, use_global_device_ids=true, to_apply=%region_11.12 | all-reduce | flops 3072 | bytes 24576 | tf_op jit(solution)/shard_map/pmax | solution.py:188
  400.9 8.5 fusion.100
  413.6 15.6 reduce-scatter.33.cloned.1.call-done
  464.5 8.5 fusion.2
  475.9 14.0 all-gather
  503.5 15.9 all_gather.14
  521.4 14.0 all-gather.1
  562.0 10.9 fusion.90
  572.9 9.6 copy.303
  589.8 13.0 multiply_convert_fusion.1
  610.2 9.7 copy.300
  733.0 10.9 pad_maximum_fusion.2
  782.5 10.7 multiply_reduce_fusion.3
  808.9 77.5 %reduce-scatter.41.cloned.1.call-done = f32[2,96,2304]{2,1,0:T(8,128)} async-done(((f32[2,768,2304]{2,1,0:T(8,128)}), f32[2,96,2304]{2,1,0:T(8,128)}) %reduce-scatter.41.cloned.1.call-update) | async-done | bytes 1769488 | tf_op jit(solution)/shard_map/reduce_scatter | solution.py:425
  886.4 188.8 %reduce-scatter.45.cloned.1.call-done = f32[2,96,3072]{2,1,0:T(8,128)} async-done(((f32[2,768,3072]{2,1,0:T(8,128)}), f32[2,96,3072]{2,1,0:T(8,128)}) %reduce-scatter.45.cloned.1.call-update) | async-done | bytes 2359312 | tf_op jit(solution)/shard_map/reduce_scatter | solution.py:430
  1075.2 188.7 %reduce-scatter.47.cloned.1.call-done = f32[2,384,768]{2,1,0:T(8,128)} async-done(((f32[2,3072,768]{2,1,0:T(8,128)}), f32[2,384,768]{2,1,0:T(8,128)}) %reduce-scatter.47.cloned.1.call-update) | async-done | bytes 2359312 | tf_op jit(solution)/shard_map/reduce_scatter | solution.py:432
  1264.6 9.1 add_convert_fusion.4
  1282.9 10.0 collective-permute-done.1
  1300.8 26.1 %reduce-scatter.57.cloned.1.call-done = f32[96,2]{1,0:T(8,128)} async-done(((f32[768,2]{1,0:T(8,128)}), f32[96,2]{1,0:T(8,128)}) %reduce-scatter.57.cloned.1.call-update) | async-done | bytes 784
  1327.8 30.3 %reduce-scatter.59.cloned.1.call-done = f32[96,2]{1,0:T(8,128)} async-done(((f32[768,2]{1,0:T(8,128)}), f32[96,2]{1,0:T(8,128)}) %reduce-scatter.59.cloned.1.call-update) | async-done | bytes 784
  1359.0 30.1 %reduce-scatter.63.cloned.1.call-done = f32[96,2]{1,0:T(8,128)} async-done(((f32[768,2]{1,0:T(8,128)}), f32[96,2]{1,0:T(8,128)}) %reduce-scatter.63.cloned.1.call-update) | async-done | bytes 784
  1390.0 34.3 %reduce-scatter.61.cloned.1.call-done = f32[384,2]{1,0:T(8,128)} async-done(((f32[3072,2]{1,0:T(8,128)}), f32[384,2]{1,0:T(8,128)}) %reduce-scatter.61.cloned.1.call-update) | async-done | bytes 3088
  1428.6 27.2 %reduce-scatter.51.cloned.1.call-done = f32[96,2]{1,0:T(8,128)} async-done(((f32[768,2]{1,0:T(8,128)}), f32[96,2]{1,0:T(8,128)}) %reduce-scatter.51.cloned.1.call-update) | async-done | bytes 784
  1456.7 30.1 %reduce-scatter.53.cloned.1.call-done = f32[96,2]{1,0:T(8,128)} async-done(((f32[768,2]{1,0:T(8,128)}), f32[96,2]{1,0:T(8,128)}) %reduce-scatter.53.cloned.1.call-update) | async-done | bytes 784
  1487.7 10.8 all-reduce
  1498.5 143.1 %all-reduce.4.cloned.1.call-done = (f32[2,96,2304]{2,1,0:T(8,128)}, f32[2,96,768]{2,1,0:T(8,128)}, f32[2,96,3072]{2,1,0:T(8,128)}, f32[2,384,768]{2,1,0:T(8,128)}) async-done(((f32[2,96,2304]{2,1,0:T(8,128)}, f32[2,96,768]{2,1,0:T(8,128)}, f32[2,96,3072]{2,1,0:T(8,128)}, f32[2,384,768]{2,1,0:T(8,128)}), (f32[2,96,2304]{2,1,0:T(8,128)}, f32[2,96,768]{2,1,0:T(8,128)}, f32[2,96,3072]{2,1,0:T(8,128)}, ...) | async-done | bytes 7077904 | tf_op jit(solution)/shard_map/psum | solution.py:447
  (587 shorter events, 572.7 us)
Async XLA Ops:
  7.2 149.1 %all-gather.4.cloned.1.call-start = ((), (), s32[]{:S(2)}) async-start(), calls=%async_computation.16 | async-start | bytes 1327104 | tf_op jit(solution)/shard_map/all_gather | solution.py:113
  9.7 21.9 %collective-permute-start = (bf16[6,84,768]{2,1,0:T(8,128)(2,1)}, bf16[6,84,768]{2,1,0:T(8,128)(2,1)S(1)}, u32[]{:S(2)}, u32[]{:S(2)}) collective-permute-start(bf16[6,84,768]{2,1,0:T(8,128)(2,1)} %get-tuple-element.145), channel_id=1, source_target_pairs={{1,0},{2,1},{3,2},{4,3},{5,4},{6,5},{7,6},{0,7},{9,8},{10,9},{11,1... | collective-permute-start | bytes 2322440 | tf_op jit(solution)/shard_map/ppermute | solution.py:17
  21.1 388.3 %reduce-scatter.49.cloned.1.call-start = ((), (), s32[]{:S(2)}) async-start(), calls=%async_computation.25 | async-start | bytes 147456
  22.5 117.5 %collective-permute-start.2 = (bf16[6,84,768]{2,1,0:T(8,128)(2,1)}, bf16[6,84,768]{2,1,0:T(8,128)(2,1)}, u32[]{:S(2)}, u32[]{:S(2)}) collective-permute-start(bf16[6,84,768]{2,1,0:T(8,128)(2,1)} %get-tuple-element.143), channel_id=1, source_target_pairs={{1,0},{2,1},{3,2},{4,3},{5,4},{6,5},{7,6},{0,7},{9,8},{10,9},{11,1... | collective-permute-start | bytes 2322440 | tf_op jit(solution)/shard_map/ppermute | solution.py:17
  25.3 161.5 %copy-start.33 = (pred[7,144,144]{1,2,0:T(8,128)(4,1)}, pred[7,144,144]{1,2,0:T(8,128)(4,1)S(1)}, u32[]{:S(2)}) copy-start(pred[7,144,144]{1,2,0:T(8,128)(4,1)S(1)} %broadcast_compare_fusion) | copy-start | bytes 435460
  26.7 146.3 %copy-start.126 = (pred[256]{0:T(512)(128)(4,1)}, pred[256]{0:T(512)(128)(4,1)S(1)}, u32[]{:S(2)}) copy-start(pred[256]{0:T(512)(128)(4,1)S(1)} %fusion.211) | copy-start | bytes 772
  28.9 200.6 %copy-start.88 = (f32[768]{0:T(1024)}, f32[768]{0:T(1024)S(1)}, u32[]{:S(2)}) copy-start(f32[768]{0:T(1024)S(1)} %get-tuple-element.100) | copy-start | bytes 9220
  28.9 264.2 %copy-start.84 = (f32[768]{0:T(1024)}, f32[768]{0:T(1024)S(1)}, u32[]{:S(2)}) copy-start(f32[768]{0:T(1024)S(1)} %get-tuple-element.189) | copy-start | bytes 9220
  81.5 79.1 %copy-start.5 = (bf16[7,144,12,64]{1,3,0,2:T(8,128)(2,1)}, bf16[7,144,12,64]{1,3,0,2:T(8,128)(2,1)S(1)}, u32[]{:S(2)}) copy-start(bf16[7,144,12,64]{1,3,0,2:T(8,128)(2,1)S(1)} %copy.266) | copy-start | bytes 4644868
  223.9 69.2 %copy-start.3 = (f32[1008,768]{1,0:T(8,128)}, f32[1008,768]{1,0:T(8,128)S(1)}, u32[]{:S(2)}) copy-start(f32[1008,768]{1,0:T(8,128)S(1)} %get-tuple-element.165) | copy-start | bytes 9289732
  347.7 81.5 %reduce-scatter.33.cloned.1.call-start = ((), (), s32[]{:S(2)}) async-start(), calls=%async_computation.17 | async-start | bytes 884736 | tf_op jit(solution)/shard_map/reduce_scatter | solution.py:196
  399.3 326.8 %reduce-scatter.39.cloned.1.call-start = ((), (), s32[]{:S(2)}) async-start(), calls=%async_computation.20 | async-start | bytes 884736 | tf_op jit(solution)/shard_map/reduce_scatter | solution.py:385
  464.4 262.6 %reduce-scatter.37.cloned.1.call-start = ((), (), s32[]{:S(2)}) async-start(), calls=%async_computation.19 | async-start | bytes 884736 | tf_op jit(solution)/shard_map/reduce_scatter | solution.py:384
  503.4 224.5 %reduce-scatter.35.cloned.1.call-start = ((), (), s32[]{:S(2)}) async-start(), calls=%async_computation.18 | async-start | bytes 884736 | tf_op jit(solution)/shard_map/reduce_scatter | solution.py:383
  547.6 261.3 %reduce-scatter.43.cloned.1.call-start = ((), (), s32[]{:S(2)}) async-start(), calls=%async_computation.22 | async-start | bytes 5308416 | tf_op jit(solution)/shard_map/reduce_scatter | solution.py:426
  554.4 332.0 %reduce-scatter.41.cloned.1.call-start = ((), (), s32[]{:S(2)}) async-start(), calls=%async_computation.21 | async-start | bytes 15925248 | tf_op jit(solution)/shard_map/reduce_scatter | solution.py:425
  744.0 331.2 %reduce-scatter.45.cloned.1.call-start = ((), (), s32[]{:S(2)}) async-start(), calls=%async_computation.23 | async-start | bytes 21233664 | tf_op jit(solution)/shard_map/reduce_scatter | solution.py:430
  762.5 501.4 %reduce-scatter.47.cloned.1.call-start = ((), (), s32[]{:S(2)}) async-start(), calls=%async_computation.24 | async-start | bytes 21233664 | tf_op jit(solution)/shard_map/reduce_scatter | solution.py:432
  779.4 520.5 %reduce-scatter.55.cloned.1.call-start = ((), (), s32[]{:S(2)}) async-start(), calls=%async_computation.28 | async-start | bytes 442368
  793.2 533.7 %reduce-scatter.57.cloned.1.call-start = ((), (), s32[]{:S(2)}) async-start(), calls=%async_computation.29 | async-start | bytes 442368
  794.3 563.9 %reduce-scatter.59.cloned.1.call-start = ((), (), s32[]{:S(2)}) async-start(), calls=%async_computation.30 | async-start | bytes 442368
  795.3 593.8 %reduce-scatter.63.cloned.1.call-start = ((), (), s32[]{:S(2)}) async-start(), calls=%async_computation.32 | async-start | bytes 442368
  796.4 628.0 %reduce-scatter.61.cloned.1.call-start = ((), (), s32[]{:S(2)}) async-start(), calls=%async_computation.31 | async-start | bytes 1769472
  799.3 656.5 %reduce-scatter.51.cloned.1.call-start = ((), (), s32[]{:S(2)}) async-start(), calls=%async_computation.26 | async-start | bytes 442368
  807.1 679.8 %reduce-scatter.53.cloned.1.call-start = ((), (), s32[]{:S(2)}) async-start(), calls=%async_computation.27 | async-start | bytes 442368
  808.8 832.8 %all-reduce.4.cloned.1.call-start = ((), (), s32[]{:S(2)}) async-start(), calls=%async_computation.33 | async-start | bytes 14155776 | tf_op jit(solution)/shard_map/psum | solution.py:447
  1277.3 15.6 collective-permute-start.1
  1282.5 142.9 %collective-permute-start.3 = (bf16[6,84,768]{2,1,0:T(8,128)(2,1)}, bf16[6,84,768]{2,1,0:T(8,128)(2,1)}, u32[]{:S(2)}, u32[]{:S(2)}) collective-permute-start(bf16[6,84,768]{2,1,0:T(8,128)(2,1)} %slice.285), channel_id=1, source_target_pairs={{7,0},{0,1},{1,2},{2,3},{3,4},{4,5},{5,6},{6,7},{15,8},{8,9},{9,10... | collective-permute-start | bytes 2322440 | tf_op jit(solution)/shard_map/ppermute | solution.py:17
  1299.9 128.0 %copy-start.57 = (f32[32,768]{1,0:T(8,128)S(1)}, f32[32,768]{1,0:T(8,128)}, u32[]{:S(2)}) copy-start(f32[32,768]{1,0:T(8,128)} %copy-done.56) | copy-start | bytes 294916
  1299.9 128.0 %copy-start.107 = (f32[32]{0:T(128)S(1)}, f32[32]{0:T(128)}, u32[]{:S(2)}) copy-start(f32[32]{0:T(128)} %copy-done.105) | copy-start | bytes 388
  1299.9 128.0 %copy-start.115 = (f32[32]{0:T(128)S(1)}, f32[32]{0:T(128)}, u32[]{:S(2)}) copy-start(f32[32]{0:T(128)} %copy-done.113) | copy-start | bytes 388
  1299.9 128.0 %copy-start.128 = (f32[32]{0:T(128)S(1)}, f32[32]{0:T(128)}, u32[]{:S(2)}) copy-start(f32[32]{0:T(128)} %copy-done.127) | copy-start | bytes 388
  (127 other events, 995.9 us)
Sparse Core Ops, SparseCore 0:
  21.2 23.3 all-gather.3
  347.8 28.3 reduce-scatter.48
  399.4 29.7 reduce-scatter.32
  464.5 29.6 reduce-scatter.38
  503.5 30.2 reduce-scatter.36
  547.7 29.5 reduce-scatter.34
  579.7 53.2 reduce-scatter.42
  744.1 142.2 reduce-scatter.40
  888.9 186.3 reduce-scatter.44
  1077.6 186.3 reduce-scatter.46
  1266.3 29.7 reduce-scatter.54
  1298.2 28.7 reduce-scatter.56
  1329.3 28.7 reduce-scatter.58
  1360.3 28.8 reduce-scatter.62
  1392.0 32.3 reduce-scatter.60
  1427.1 28.6 reduce-scatter.50
  1457.9 28.8 reduce-scatter.52
  1491.0 150.6 all-reduce.3
where the time goes:
time: 1670 us; the launch traced here: 1660 us
  waiting for transfers between devices  802 us (48%)
  local copies, waits for them, and re-layouts  341 us (20%)
  matrix products  291 us (17%)
  other arithmetic  117 us (7%)
  blocking collectives  80.6 us (5%)
  between operations  17.3 us (1%)
    reduce_scatter x1, waiting for transfers between devices, body(): lax.psum_scatter(up_grad, 'strip', scatter_dimension=1, tiled=True)  189 us
    reduce_scatter x1, waiting for transfers between devices, body(): lax.psum_scatter(down_grad, 'strip', scatter_dimension=1, tiled=True)  189 us
    unnamed x26, waiting for transfers between devices  179 us
    psum x1, waiting for transfers between devices, body(): lax.psum((gain_one, bias_one, qkv_grad, out_grad, obias_grad, gain_two, b...  143 us
    reduce_scatter x1, waiting for transfers between devices, body(): lax.psum_scatter(qkv_grad, 'strip', scatter_dimension=1, tiled=True)  77.5 us
    dot_general x8, matrix products, matmul(): return jnp.dot(operand_a, operand_b, preferred_element_type=jnp.float32)  68.6 us
    dot_general x8, matrix products, times_t(): lax.dot_general(operand_a, operand_b, (((1,), (1,)), ((), ())), preferred...  55.9 us
    unnamed x292, local copies, waits for them, and re-layouts  42.9 us
  transfers between devices with their start and end apart: 22, of which 12 were waited for; matrix products, arithmetic and copies ran while one was open for 32% of the time, Pallas kernels for 0%

commit v1 on v0

v1 whole, which is shorter than its diff:
```python
import functools

import jax
import jax.numpy as jnp
from jax import lax
from jax.experimental import pallas as pl
from jax.experimental.pallas import tpu as pltpu
from jax.sharding import PartitionSpec as P

HEADS = 12
WIN = 12
SHIFT = 6
CELLS = WIN * WIN
PAIR = 128
MASKED = -1000000000.0
VMEM_LIMIT = 56 * 1024 * 1024

bf16 = jnp.bfloat16
f32 = jnp.float32


def params():
    return pltpu.CompilerParams(vmem_limit_bytes=VMEM_LIMIT)


def row_block(rows):
    for size in range(336, 15, -16):
        if rows % size == 0:
            return size
    return rows


def dot_nn(a, b):
    return lax.dot_general(a, b, (((1,), (0,)), ((), ())), preferred_element_type=f32)


def dot_nt(a, b):
    return lax.dot_general(a, b, (((1,), (1,)), ((), ())), preferred_element_type=f32)


def dot_tn(a, b):
    return lax.dot_general(a, b, (((0,), (0,)), ((), ())), preferred_element_type=f32)


def cost(flops, moved, special=0):
    return pl.CostEstimate(flops=int(flops), bytes_accessed=int(moved), transcendentals=int(special))


def whole(shape):
    return pl.BlockSpec(shape, lambda *_: (0,) * len(shape))


def normalised(values):
    center = values - jnp.mean(values, -1, keepdims=True)
    spread = jnp.mean(center * center, -1, keepdims=True)
    rstd = lax.rsqrt(spread + 1e-05)
    return center * rstd, rstd


def norm_back(grad, hat, rstd, gain):
    scaled = grad * gain
    mean_one = jnp.mean(scaled, -1, keepdims=True)
    mean_two = jnp.mean(scaled * hat, -1, keepdims=True)
    return rstd * (scaled - mean_one - hat * mean_two)


def qkv_kernel(stream, x_ref, gain_ref, bias_ref, w_ref, a_ref, out_ref):
    rows, width = x_ref.shape
    block = row_block(rows)

    @pl.when(pl.program_id(0) == 0)
    def _():
        @pl.loop(0, rows // block)
        def _(i):
            at = pl.ds(pl.multiple_of(i * block, block), block)
            hat, _ = normalised(x_ref[at, :].astype(f32))
            a_ref[at, :] = (
                hat * gain_ref[stream : stream + 1, :] + bias_ref[stream : stream + 1, :]
            ).astype(bf16)

    @pl.loop(0, rows // block)
    def _(i):
        at = pl.ds(pl.multiple_of(i * block, block), block)
        out_ref[at, :] = dot_nn(a_ref[at, :], w_ref[...]).astype(bf16)


def norm_qkv(x, gain, bias, weight, stream):
    rows, width = x.shape
    full = weight.shape[-1]
    return pl.pallas_call(
        functools.partial(qkv_kernel, stream),
        grid=(full // width,),
        in_specs=[
            whole((rows, width)),
            whole(gain.shape),
            whole(bias.shape),
            pl.BlockSpec((None, width, width), lambda j: (stream, 0, j)),
        ],
        out_specs=[whole((rows, width)), pl.BlockSpec((rows, width), lambda j: (0, j))],
        out_shape=[
            jax.ShapeDtypeStruct((rows, width), bf16),
            jax.ShapeDtypeStruct((rows, full), bf16),
        ],
        compiler_params=params(),
        cost_estimate=cost(2 * rows * width * full, 2 * rows * (2 * width + full) + 2 * width * full),
        name="norm_qkv",
    )(x, gain, bias, weight)


def first_half(shape):
    return lax.broadcasted_iota(jnp.int32, shape, len(shape) - 1) < PAIR // 2


def stacked(block):
    left = first_half(block.shape)
    zero = jnp.zeros_like(block)
    return jnp.concatenate([jnp.where(left, block, zero), jnp.where(left, zero, block)], 0)


def unstacked(turned, rows):
    upright = turned.T
    return jnp.where(first_half((rows, PAIR)), upright[:rows], upright[rows:])


def query_forward_kernel(
    windows, qq_ref, k_ref, v_ref, ko_ref, vo_ref, bias_ref, out_ref, lse_ref, s_ref
):
    queries = qq_ref.shape[0]
    own = ko_ref.shape[0]
    scaled = stacked(qq_ref[...] * 0.125)
    cells = windows * CELLS
    bias = bias_ref[...]
    score = dot_nt(ko_ref[...], scaled) + jnp.concatenate([bias, bias], 1)
    s_ref[cells : cells + own, :] = score
    top = jnp.max(score, 0, keepdims=True)
    for w in range(windows):
        score = dot_nt(k_ref[w * CELLS : (w + 1) * CELLS, :], scaled)
        s_ref[w * CELLS : (w + 1) * CELLS, :] = score
        top = jnp.maximum(top, jnp.max(score, 0, keepdims=True))
    prob = jnp.exp(s_ref[cells : cells + own, :] - top)
    total = jnp.sum(prob, 0, keepdims=True)
    mixed = dot_nn(vo_ref[...].T, prob.astype(bf16))
    for w in range(windows):
        prob = jnp.exp(s_ref[w * CELLS : (w + 1) * CELLS, :] - top)
        total = total + jnp.sum(prob, 0, keepdims=True)
        mixed = mixed + dot_nn(v_ref[w * CELLS : (w + 1) * CELLS, :].T, prob.astype(bf16))
    out_ref[...] = unstacked(mixed * (1.0 / total), queries).astype(bf16)
    lse_ref[...] = top + jnp.log(total)


def query_forward(query_qkv, own_qkv, vis_qkv, self_bias):
    cells = vis_qkv.shape[0]
    queries = query_qkv.shape[0]
    own = own_qkv.shape[0]
    width = query_qkv.shape[1] // 3
    pairs = width // PAIR
    keys = cells + own

    def part(rows, j):
        return pl.BlockSpec((rows, PAIR), lambda p, j=j: (0, j * pairs + p))

    return pl.pallas_call(
        functools.partial(query_forward_kernel, cells // CELLS),
        grid=(pairs,),
        in_specs=[
            part(queries, 0),
            part(cells, 1),
            part(cells, 2),
            part(own, 1),
            part(own, 2),
            whole(self_bias.shape),
        ],
        out_specs=[part(queries, 0), pl.BlockSpec((None, 1, 2 * queries), lambda p: (p, 0, 0))],
        out_shape=[
            jax.ShapeDtypeStruct((queries, width), bf16),
            jax.ShapeDtypeStruct((pairs, 1, 2 * queries), f32),
        ],
        scratch_shapes=[pltpu.VMEM((keys, 2 * queries), f32)],
        compiler_params=params(),
        cost_estimate=cost(
            4 * 2 * queries * keys * width, 4 * cells * width, 2 * queries * keys * pairs
        ),
        name="query_forward",
    )(query_qkv, vis_qkv, vis_qkv, own_qkv, own_qkv, self_bias)


def window_forward_kernel(
    windows, q_ref, k_ref, v_ref, kq_ref, vq_ref, row_ref, col_ref, open_ref, out_ref, lse_ref
):
    kq = kq_ref[...]
    vq_turned = vq_ref[...].T
    closed = open_ref[...]
    for w in range(windows):
        at = slice(w * CELLS, (w + 1) * CELLS)
        scaled = stacked(q_ref[at, :] * 0.125)
        near = dot_nt(k_ref[at, :], scaled)
        near = jnp.where(col_ref[w] == row_ref[w], near, MASKED)
        far = dot_nt(kq, scaled) + closed
        top = jnp.maximum(jnp.max(near, 0, keepdims=True), jnp.max(far, 0, keepdims=True))
        near = jnp.exp(near - top)
        far = jnp.exp(far - top)
        total = jnp.sum(near, 0, keepdims=True) + jnp.sum(far, 0, keepdims=True)
        mixed = dot_nn(v_ref[at, :].T, near.astype(bf16)) + dot_nn(vq_turned, far.astype(bf16))
        out_ref[at, :] = unstacked(mixed * (1.0 / total), CELLS).astype(bf16)
        lse_ref[w : w + 1, :] = top + jnp.log(total)


def window_forward(vis_qkv, query_qkv, region_row, region_col, closed):
    cells = vis_qkv.shape[0]
    queries = query_qkv.shape[0]
    width = vis_qkv.shape[1] // 3
    pairs = width // PAIR
    windows = cells // CELLS

    def part(rows, j):
        return pl.BlockSpec((rows, PAIR), lambda p, j=j: (0, j * pairs + p))

    return pl.pallas_call(
        functools.partial(window_forward_kernel, windows),
        grid=(pairs,),
        in_specs=[
            part(cells, 0),
            part(cells, 1),
            part(cells, 2),
            part(queries, 1),
            part(queries, 2),
            whole(region_row.shape),
            whole(region_col.shape),
            whole(closed.shape),
        ],
        out_specs=[
            part(cells, 0),
            pl.BlockSpec((None, windows, 2 * CELLS), lambda p: (p, 0, 0)),
        ],
        out_shape=[
            jax.ShapeDtypeStruct((cells, width), bf16),
            jax.ShapeDtypeStruct((pairs, windows, 2 * CELLS), f32),
        ],
        compiler_params=params(),
        cost_estimate=cost(
            8 * cells * (CELLS + queries) * width,
            8 * cells * width,
            2 * pairs * cells * (CELLS + queries),
        ),
        name="window_forward",
    )(vis_qkv, vis_qkv, vis_qkv, query_qkv, query_qkv, region_row, region_col, closed)


def attention_backward_kernel(
    windows,
    q_ref,
    k_ref,
    v_ref,
    do_ref,
    qq_ref,
    kq_ref,
    vq_ref,
    doq_ref,
    ko_ref,
    vo_ref,
    row_ref,
    col_ref,
    open_ref,
    bias_ref,
    lse_ref,
    lseq_ref,
    deltaq_ref,
    dq_ref,
    dk_ref,
    dv_ref,
    dqq_ref,
    dkq_ref,
    dvq_ref,
    dko_ref,
    dvo_ref,
    sumq_ref,
):
    queries = qq_ref.shape[0]
    kq = kq_ref[...]
    vq = vq_ref[...]
    kq_turned = kq.T
    closed = open_ref[...]
    scaled_q = stacked(qq_ref[...] * 0.125)
    grad_q = stacked(doq_ref[...])
    lse_q = lseq_ref[...]
    delta_q = deltaq_ref[...]

    bias = bias_ref[...]
    prob = jnp.exp(dot_nt(ko_ref[...], scaled_q) + jnp.concatenate([bias, bias], 1) - lse_q)
    dscore = (prob * (dot_nt(vo_ref[...], grad_q) - delta_q)).astype(bf16)
    dko_ref[...] = dot_nn(dscore, scaled_q)
    dvo_ref[...] = dot_nn(prob.astype(bf16), grad_q)
    sumq_ref[...] = dot_nn(ko_ref[...].T, dscore)

    for w in range(windows):
        at = slice(w * CELLS, (w + 1) * CELLS)
        k_win = k_ref[at, :]
        v_win = v_ref[at, :]
        k_turned = k_win.T
        scaled = stacked(q_ref[at, :] * 0.125)
        grad = stacked(do_ref[at, :])
        lse = lse_ref[w : w + 1, :]
        near = dot_nt(k_win, scaled)
        near = jnp.exp(jnp.where(col_ref[w] == row_ref[w], near, MASKED) - lse)
        far = jnp.exp(dot_nt(kq, scaled) + closed - lse)
        near_t = near * dot_nt(v_win, grad)
        far_t = far * dot_nt(vq, grad)
        delta = jnp.sum(near_t, 0, keepdims=True) + jnp.sum(far_t, 0, keepdims=True)
        near_d = (near_t - near * delta).astype(bf16)
        far_d = (far_t - far * delta).astype(bf16)
        turned = dot_nn(k_turned, near_d) + dot_nn(kq_turned, far_d)
        dq_ref[at, :] = (unstacked(turned, CELLS) * 0.125).astype(bf16)
        dkq = dot_nn(far_d, scaled)
        dvq = dot_nn(far.astype(bf16), grad)
        if w == 0:
            dkq_ref[...] = dkq
            dvq_ref[...] = dvq
        else:
            dkq_ref[...] += dkq
            dvq_ref[...] += dvq

        seen = jnp.exp(dot_nt(k_win, scaled_q) - lse_q)
        seen_d = (seen * (dot_nt(v_win, grad_q) - delta_q)).astype(bf16)
        sumq_ref[...] += dot_nn(k_turned, seen_d)
        dk_ref[at, :] = (dot_nn(near_d, scaled) + dot_nn(seen_d, scaled_q)).astype(bf16)
        dv_ref[at, :] = (
            dot_nn(near.astype(bf16), grad) + dot_nn(seen.astype(bf16), grad_q)
        ).astype(bf16)
    dqq_ref[...] = unstacked(sumq_ref[...], queries) * 0.125


def attention_backward(
    vis_qkv,
    query_qkv,
    own_qkv,
    grad,
    grad_q,
    region_row,
    region_col,
    closed,
    self_bias,
    lse,
    lse_q,
    delta_q,
    first,
    count,
):
    cells = vis_qkv.shape[0]
    queries = query_qkv.shape[0]
    own = own_qkv.shape[0]
    width = vis_qkv.shape[1] // 3
    pairs = width // PAIR
    windows = cells // CELLS

    def part(rows, j):
        return pl.BlockSpec((rows, PAIR), lambda p, j=j: (0, j * pairs + first + p))

    def result(rows):
        return pl.BlockSpec((rows, PAIR), lambda p: (0, p))

    def stats(array):
        return pl.BlockSpec((None,) + array.shape[1:], lambda p: (first + p, 0, 0))

    span = count * PAIR
    return pl.pallas_call(
        functools.partial(attention_backward_kernel, windows),
        grid=(count,),
        in_specs=[
            part(cells, 0),
            part(cells, 1),
            part(cells, 2),
            part(cells, 0),
            part(queries, 0),
            part(queries, 1),
            part(queries, 2),
            part(queries, 0),
            part(own, 1),
            part(own, 2),
            whole(region_row.shape),
            whole(region_col.shape),
            whole(closed.shape),
            whole(self_bias.shape),
            stats(lse),
            stats(lse_q),
            stats(delta_q),
        ],
        out_specs=[result(cells)] * 3 + [result(queries)] * 3 + [result(own)] * 2,
        out_shape=[jax.ShapeDtypeStruct((cells, span), bf16)] * 3
        + [jax.ShapeDtypeStruct((queries, span), f32)] * 3
        + [jax.ShapeDtypeStruct((own, span), f32)] * 2,
        scratch_shapes=[pltpu.VMEM((PAIR, 2 * queries), f32)],
        compiler_params=params(),
        cost_estimate=cost(
            20 * cells * (CELLS + 2 * queries) * span,
            14 * cells * span,
            2 * count * cells * (CELLS + 2 * queries),
        ),
        name="attention_backward",
    )(
        vis_qkv,
        vis_qkv,
        vis_qkv,
        grad,
        query_qkv,
        query_qkv,
        query_qkv,
        grad_q,
        own_qkv,
        own_qkv,
        region_row,
        region_col,
        closed,
        self_bias,
        lse,
        lse_q,
        delta_q,
    )


def gelu_pair(z):
    size = jnp.abs(z)
    t = 1.0 / (1.0 + (0.3275911 * 0.7071067811865476) * size)
    bell = jnp.exp(-0.5 * z * z)
    poly = 0.5 * 1.061405429
    for term in (-1.453152027, 1.421413741, -0.284496736, 0.254829592):
        poly = poly * t + 0.5 * term
    tail = poly * t * bell
    below = jnp.where(z >= 0, 1.0 - tail, tail)
    return z * below, below + z * bell * 0.3989422804014327


def ffn_forward_kernel(
    stream,
    x_ref,
    o_ref,
    wo_ref,
    bo_ref,
    gain_ref,
    bias_ref,
    wu_ref,
    bu_ref,
    wd_ref,
    bd_ref,
    x1_ref,
    b_ref,
    hid_ref,
    slope_ref,
    out_ref,
    sum_ref,
):
    rows, width = x_ref.shape
    block = row_block(rows)
    step = pl.program_id(0)
    row = slice(stream, stream + 1)

    @pl.when(step == 0)
    def _():
        @pl.loop(0, rows // block)
        def _(i):
            at = pl.ds(pl.multiple_of(i * block, block), block)
            x1 = x_ref[at, :].astype(f32) + dot_nn(o_ref[at, :], wo_ref[...]) + bo_ref[row, :]
            x1_ref[at, :] = x1
            hat, _ = normalised(x1)
            b_ref[at, :] = (hat * gain_ref[row, :] + bias_ref[row, :]).astype(bf16)
            sum_ref[at, :] = x1 + bd_ref[row, :]

    @pl.loop(0, rows // block)
    def _(i):
        at = pl.ds(pl.multiple_of(i * block, block), block)
        z = dot_nn(b_ref[at, :], wu_ref[...]) + bu_ref[row, :]
        hidden, slope = gelu_pair(z)
        hidden = hidden.astype(bf16)
        hid_ref[at, :] = hidden
        slope_ref[at, :] = slope.astype(bf16)
        sum_ref[at, :] += dot_nn(hidden, wd_ref[...])

    @pl.when(step == pl.num_programs(0) - 1)
    def _():
        out_ref[...] = sum_ref[...].astype(bf16)


def ffn_forward(x, attended, out_w, out_b, gain, bias, up_w, up_b, down_w, down_b, stream):
    rows, width = x.shape
    hidden = up_w.shape[-1]
    chunk = 512
    return pl.pallas_call(
        functools.partial(ffn_forward_kernel, stream),
        grid=(hidden // chunk,),
        in_specs=[
            whole((rows, width)),
            whole((rows, width)),
            pl.BlockSpec((None, width, width), lambda f: (stream, 0, 0)),
            whole(out_b.shape),
            whole(gain.shape),
            whole(bias.shape),
            pl.BlockSpec((None, width, chunk), lambda f: (stream, 0, f)),
            pl.BlockSpec((2, chunk), lambda f: (0, f)),
            pl.BlockSpec((None, chunk, width), lambda f: (stream, f, 0)),
            whole(down_b.shape),
        ],
        out_specs=[
            whole((rows, width)),
            whole((rows, width)),
            pl.BlockSpec((rows, chunk), lambda f: (0, f)),
            pl.BlockSpec((rows, chunk), lambda f: (0, f)),
            whole((rows, width)),
        ],
        out_shape=[
            jax.ShapeDtypeStruct((rows, width), f32),
            jax.ShapeDtypeStruct((rows, width), bf16),
            jax.ShapeDtypeStruct((rows, hidden), bf16),
            jax.ShapeDtypeStruct((rows, hidden), bf16),
            jax.ShapeDtypeStruct((rows, width), bf16),
        ],
        scratch_shapes=[pltpu.VMEM((rows, width), f32)],
        compiler_params=params(),
        cost_estimate=cost(
            2 * rows * width * (2 * hidden + width),
            4 * width * hidden + 4 * rows * hidden + 12 * rows * width,
            2 * rows * hidden,
        ),
        name="ffn_forward",
    )(x, attended, out_w, out_b, gain, bias, up_w, up_b, down_w, down_b)


def ffn_backward_kernel(
    stream,
    g_ref,
    slope_ref,
    x1_ref,
    wd_ref,
    wu_ref,
    wo_ref,
    gain_ref,
    dz_ref,
    upb_ref,
    dx1_ref,
    du_ref,
    do_ref,
    sums_ref,
    sum_ref,
):
    rows, width = g_ref.shape
    block = row_block(rows)
    step = pl.program_id(0)
    row = slice(stream, stream + 1)

    @pl.when(step == 0)
    def _():
        sum_ref[...] = jnp.zeros_like(sum_ref)

    upb_ref[...] = jnp.zeros_like(upb_ref)

    @pl.loop(0, rows // block)
    def _(i):
        at = pl.ds(pl.multiple_of(i * block, block), block)
        dz = dot_nt(g_ref[at, :], wd_ref[...]) * slope_ref[at, :].astype(f32)
        low = dz.astype(bf16)
        dz_ref[at, :] = low
        upb_ref[...] += jnp.sum(dz, 0, keepdims=True)
        sum_ref[at, :] += dot_nt(low, wu_ref[...])

    @pl.when(step == pl.num_programs(0) - 1)
    def _():
        sums_ref[...] = jnp.zeros_like(sums_ref)

        @pl.loop(0, rows // block)
        def _(i):
            at = pl.ds(pl.multiple_of(i * block, block), block)
            hat, rstd = normalised(x1_ref[at, :])
            db = sum_ref[at, :]
            g = g_ref[at, :].astype(f32)
            dx1 = g + norm_back(db, hat, rstd, gain_ref[row, :])
            dx1_ref[at, :] = dx1
            du = dx1.astype(bf16)
            du_ref[at, :] = du
            do_ref[at, :] = dot_nt(du, wo_ref[...]).astype(bf16)
            sums_ref[0:1, :] += jnp.sum(db * hat, 0, keepdims=True)
            sums_ref[1:2, :] += jnp.sum(db, 0, keepdims=True)
            sums_ref[2:3, :] += jnp.sum(dx1, 0, keepdims=True)
            sums_ref[3:4, :] += jnp.sum(g, 0, keepdims=True)


def ffn_backward(g, slope, x1, down_w, up_w, out_w, gain, stream):
    rows, width = g.shape
    hidden = up_w.shape[-1]
    chunk = 512
    return pl.pallas_call(
        functools.partial(ffn_backward_kernel, stream),
        grid=(hidden // chunk,),
        in_specs=[
            whole((rows, width)),
            pl.BlockSpec((rows, chunk), lambda f: (0, f)),
            whole((rows, width)),
            pl.BlockSpec((None, chunk, width), lambda f: (stream, f, 0)),
            pl.BlockSpec((None, width, chunk), lambda f: (stream, 0, f)),
            pl.BlockSpec((None, width, width), lambda f: (stream, 0, 0)),
            whole(gain.shape),
        ],
        out_specs=[
            pl.BlockSpec((rows, chunk), lambda f: (0, f)),
            pl.BlockSpec((1, chunk), lambda f: (0, f)),
            whole((rows, width)),
            whole((rows, width)),
            whole((rows, width)),
            whole((8, width)),
        ],
        out_shape=[
            jax.ShapeDtypeStruct((rows, hidden), bf16),
            jax.ShapeDtypeStruct((1, hidden), f32),
            jax.ShapeDtypeStruct((rows, width), f32),
            jax.ShapeDtypeStruct((rows, width), bf16),
            jax.ShapeDtypeStruct((rows, width), bf16),
            jax.ShapeDtypeStruct((8, width), f32),
        ],
        scratch_shapes=[pltpu.VMEM((rows, width), f32)],
        compiler_params=params(),
        cost_estimate=cost(
            2 * rows * width * (2 * hidden + width),
            4 * width * hidden + 4 * rows * hidden + 14 * rows * width,
        ),
        name="ffn_backward",
    )(g, slope, x1, down_w, up_w, out_w, gain)


def input_kernel(stream, dq_ref, dk_ref, dv_ref, w_ref, x_ref, dx1_ref, gain_ref, out_ref, sums_ref):
    rows, width = x_ref.shape
    block = row_block(rows)
    row = slice(stream, stream + 1)
    sums_ref[...] = jnp.zeros_like(sums_ref)

    @pl.loop(0, rows // block)
    def _(i):
        at = pl.ds(pl.multiple_of(i * block, block), block)
        grad = dot_nt(dq_ref[at, :], w_ref[:, :width])
        grad = grad + dot_nt(dk_ref[at, :], w_ref[:, width : 2 * width])
        grad = grad + dot_nt(dv_ref[at, :], w_ref[:, 2 * width :])
        hat, rstd = normalised(x_ref[at, :].astype(f32))
        out_ref[at, :] = (
            dx1_ref[at, :] + norm_back(grad, hat, rstd, gain_ref[row, :])
        ).astype(bf16)
        sums_ref[0:1, :] += jnp.sum(grad * hat, 0, keepdims=True)
        sums_ref[1:2, :] += jnp.sum(grad, 0, keepdims=True)


def input_grad(dq, dk, dv, weight, x, dx1, gain, stream):
    rows, width = x.shape
    return pl.pallas_call(
        functools.partial(input_kernel, stream),
        grid=(1,),
        in_specs=[whole((rows, width))] * 3
        + [
            pl.BlockSpec((None, width, 3 * width), lambda j: (stream, 0, 0)),
            whole((rows, width)),
            whole((rows, width)),
            whole(gain.shape),
        ],
        out_specs=[whole((rows, width)), whole((8, width))],
        out_shape=[
            jax.ShapeDtypeStruct((rows, width), bf16),
            jax.ShapeDtypeStruct((8, width), f32),
        ],
        compiler_params=params(),
        cost_estimate=cost(6 * rows * width * width, 14 * rows * width + 6 * width * width),
        name="input_grad",
    )(dq, dk, dv, weight, x, dx1, gain)


def moved(block, axis, step):
    size = lax.axis_size(axis)
    return lax.ppermute(block, axis, [(i, (i + step) % size) for i in range(size)])


def other_core(block):
    size = lax.axis_size("strip")
    return lax.ppermute(block, "strip", [(i, i ^ 1) for i in range(size)])


def pick(block, index, axis=0):
    return lax.dynamic_index_in_dim(block, index, axis, keepdims=False)


def added(*blocks):
    total = blocks[0].astype(f32)
    for block in blocks[1:]:
        total = total + block.astype(f32)
    return total.astype(bf16)


def sum_cores(grad):
    core = lax.axis_index("strip") % 2
    return added(pick(grad, core, 1), other_core(pick(grad, 1 - core, 1)))


def sum_line(grad):
    size = lax.axis_size("strip") // 2
    z = lax.axis_index("strip") // 2
    blocks = [pick(grad, z)]
    for step in range(1, size):
        blocks.append(moved(pick(grad, (z + step) % size), "strip", 2 * step))
    return added(*blocks)


def sum_pages(grad):
    size = lax.axis_size("page")
    page = lax.axis_index("page")
    axis = grad.ndim - 3
    blocks = [pick(grad, page, axis)]
    for step in range(1, size):
        blocks.append(moved(pick(grad, (page + step) % size, axis), "page", step))
    return added(*blocks)


def gather_pages(block):
    size = lax.axis_size("page")
    page = lax.axis_index("page")
    blocks = [block] + [moved(block, "page", size - step) for step in range(1, size)]
    double = jnp.stack(blocks + blocks)
    return lax.dynamic_slice_in_dim(double, (size - page) % size, size, 0)


def by_strip(grad):
    strips = lax.axis_size("strip")
    return grad.reshape(strips // 2, 2, grad.shape[0] // strips, grad.shape[1])


def by_page(grad):
    pages = lax.axis_size("page")
    return grad.reshape(grad.shape[:-2] + (pages, grad.shape[-2] // pages, grad.shape[-1]))


def finished(parts):
    every = gather_pages(parts)
    every = jnp.swapaxes(every, 0, 1).astype(f32)
    return every.reshape(2, -1, every.shape[-1])


def reduce_line_first(vis_grad, query_grad):
    rows = sum_line(sum_cores(by_strip(vis_grad)))
    return finished(sum_pages(by_page(jnp.stack([rows, query_grad]))))


def reduce_pages_first(vis_grad, query_grad):
    strips = sum_cores(by_strip(vis_grad))
    both = jnp.concatenate([strips, query_grad[None]], 0)
    part = sum_pages(by_page(both))
    rows = sum_line(part[:-1])
    return finished(jnp.stack([rows, part[-1]]))


def to_windows(rows):
    across = rows.shape[1] // WIN
    rolled = jnp.roll(rows, -SHIFT, axis=1)
    return (
        rolled.reshape(WIN, across, WIN, rows.shape[-1])
        .transpose(1, 0, 2, 3)
        .reshape(-1, rows.shape[-1])
    )


def from_windows(cells, columns):
    across = columns // WIN
    rows = (
        cells.reshape(across, WIN, WIN, cells.shape[-1])
        .transpose(1, 0, 2, 3)
        .reshape(WIN, columns, cells.shape[-1])
    )
    return jnp.roll(rows, SHIFT, axis=1)


def weight_grad(left, right):
    return dot_tn(left, right).astype(bf16)


def body(
    vis_tokens,
    query_tokens,
    region_ids,
    query_mask,
    answer_len,
    norm1_gain,
    norm1_bias,
    qkv_weight,
    out_weight,
    out_bias,
    norm2_gain,
    norm2_bias,
    up_weight,
    up_bias,
    down_weight,
    down_bias,
    vis_cotangent,
    query_cotangent,
):
    strips = lax.axis_size("strip")
    strip = lax.axis_index("strip")
    local_rows, columns, features = vis_tokens.shape[1:]
    own_count = query_tokens.shape[1]
    query_count = query_mask.shape[1]
    total_rows = region_ids.shape[1]
    windows = columns // WIN
    own_start = strip * own_count

    head_rows = moved(vis_tokens[0, :SHIFT], "strip", -1)
    head_cot = moved(vis_cotangent[0, :SHIFT], "strip", -1)
    query = lax.all_gather(query_tokens[0], "strip", axis=0, tiled=True)
    query_cot = lax.all_gather(query_cotangent[0], "strip", axis=0, tiled=True)
    vis = to_windows(jnp.concatenate([vis_tokens[0, SHIFT:], head_rows], 0))
    vis_cot = to_windows(jnp.concatenate([vis_cotangent[0, SHIFT:], head_cot], 0))

    key_open = query_mask[0] > 0
    key_ids = jnp.arange(query_count, dtype=jnp.int32)
    prompt = key_ids < query_count - answer_len[0]
    closed = jnp.where(key_open & prompt, 0.0, MASKED).astype(f32)[:, None]
    own_ids = own_start + jnp.arange(own_count, dtype=jnp.int32)
    own_open = lax.dynamic_slice_in_dim(key_open, own_start, own_count)
    own_prompt = lax.dynamic_slice_in_dim(prompt, own_start, own_count)
    allowed = own_open[:, None] & (own_prompt[:, None] | (own_ids[:, None] <= key_ids[None, :]))
    self_bias = jnp.where(allowed, 0.0, MASKED).astype(f32)
    row_ids = (strip * local_rows + SHIFT + jnp.arange(local_rows, dtype=jnp.int32)) % total_rows
    region = to_windows(jnp.take(region_ids[0], row_ids, axis=0)[..., None]).reshape(windows, CELLS)
    region_row = jnp.concatenate([region, region], 1)[:, None, :]
    region_col = region[:, :, None]

    query_norm, query_qkv = norm_qkv(query, norm1_gain, norm1_bias, qkv_weight, 1)
    own_qkv = lax.dynamic_slice_in_dim(query_qkv, own_start, own_count, 0)
    vis_norm, vis_qkv = norm_qkv(vis, norm1_gain, norm1_bias, qkv_weight, 0)
    part_mix, part_lse = query_forward(query_qkv, own_qkv, vis_qkv, self_bias)
    mixes, tops = [part_mix], [part_lse]
    for step in range(1, strips):
        mixes.append(moved(part_mix, "strip", step))
        tops.append(moved(part_lse, "strip", step))
    vis_attn, vis_lse = window_forward(vis_qkv, query_qkv, region_row, region_col, closed)

    weights = (out_weight, out_bias, norm2_gain, norm2_bias, up_weight, up_bias, down_weight, down_bias)
    vis_x1, vis_b, vis_hid, vis_slope, vis_result = ffn_forward(vis, vis_attn, *weights, 0)
    vis_down = weight_grad(vis_hid, vis_cot)
    vis_dz, vis_upb, vis_dx1, vis_du, vis_do, vis_sums = ffn_backward(
        vis_cot, vis_slope, vis_x1, down_weight, up_weight, out_weight, norm2_gain, 0
    )
    vis_up = weight_grad(vis_b, vis_dz)
    vis_outg = weight_grad(vis_attn, vis_du)

    pairs = part_lse.shape[0]
    tops = jnp.stack(tops)
    top = tops.max(0)
    shares = jnp.exp(tops - top)
    total = shares.sum(0)
    query_lse = top + jnp.log(total)
    shares = (shares / total).reshape(strips, pairs, 2, query_count)
    shares = shares.transpose(0, 3, 1, 2).reshape(strips, query_count, HEADS, 1)
    mixes = jnp.stack(mixes).reshape(strips, query_count, HEADS, -1)
    query_mix = (mixes.astype(f32) * shares).sum(0).reshape(query_count, features)
    query_attn = query_mix.astype(bf16)
    query_x1, query_b, query_hid, query_slope, query_result = ffn_forward(
        query, query_attn, *weights, 1
    )
    query_dz, query_upb, query_dx1, query_du, query_do, query_sums = ffn_backward(
        query_cot, query_slope, query_x1, down_weight, up_weight, out_weight, norm2_gain, 1
    )
    query_delta = (query_do.astype(f32) * query_mix).reshape(query_count, pairs, 2, -1).sum(-1)
    query_delta = query_delta.transpose(1, 2, 0).reshape(pairs, 1, 2 * query_count)

    def own_slice(values):
        span = values.shape[1] // strips
        return lax.dynamic_slice_in_dim(values, strip * span, span, 1)

    def query_weight_grad(left, right):
        return weight_grad(own_slice(left), right)

    down_grad = reduce_line_first(vis_down, query_weight_grad(query_hid, query_cot))
    up_grad = reduce_pages_first(vis_up, query_weight_grad(query_b, query_dz))
    out_grad = reduce_line_first(vis_outg, query_weight_grad(query_attn, query_du))

    vis_dq, vis_dk, vis_dv, part_q, part_k, part_v, self_k, self_v = attention_backward(
        vis_qkv,
        query_qkv,
        own_qkv,
        vis_do,
        query_do,
        region_row,
        region_col,
        closed,
        self_bias,
        vis_lse,
        query_lse,
        query_delta,
        0,
        pairs,
    )
    part = jnp.concatenate([part_q, part_k, part_v], 1).astype(bf16)
    own_dqkv = sum_line(sum_cores(by_strip(part))).astype(f32)
    own_dqkv = own_dqkv + jnp.concatenate([jnp.zeros_like(self_k), self_k, self_v], 1)
    own_dqkv = own_dqkv.astype(bf16)
    query_dqkv = lax.all_gather(own_dqkv, "strip", axis=0, tiled=True)

    vis_qkvg = jnp.concatenate([weight_grad(vis_norm, each) for each in (vis_dq, vis_dk, vis_dv)], 1)
    qkv_grad = reduce_pages_first(vis_qkvg, query_weight_grad(query_norm, query_dqkv))

    vis_input, vis_head = input_grad(
        vis_dq, vis_dk, vis_dv, qkv_weight, vis, vis_dx1, norm1_gain, 0
    )
    own_input, own_head = input_grad(
        own_dqkv[:, :features],
        own_dqkv[:, features : 2 * features],
        own_dqkv[:, 2 * features :],
        qkv_weight,
        query_tokens[0],
        lax.dynamic_slice_in_dim(query_dx1, own_start, own_count, 0),
        norm1_gain,
        1,
    )
    own_result = lax.dynamic_slice_in_dim(query_result, own_start, own_count, 0)

    def to_rows(cells):
        grid = from_windows(cells, columns)
        tail = moved(grid[local_rows - SHIFT :], "strip", 1)
        return jnp.concatenate([tail, grid[: local_rows - SHIFT]], 0)[None]

    once = jnp.where(strip == 0, 1.0, 0.0)
    small = jnp.stack(
        [
            jnp.concatenate([vis_head[:2], vis_sums[:4], vis_upb.reshape(-1, features)], 0),
            jnp.concatenate(
                [own_head[:2], once * query_sums[:4], once * query_upb.reshape(-1, features)], 0
            ),
        ]
    )
    small = lax.psum(small, ("page", "strip"))
    gain_one, bias_one, gain_two, bias_two, obias, dbias = [own_slice(small[:, i]) for i in range(6)]
    ubias = own_slice(small[:, 6:].reshape(2, -1))

    return (
        to_rows(vis_result),
        own_result[None],
        to_rows(vis_input),
        own_input[None],
        gain_one,
        bias_one,
        qkv_grad,
        out_grad,
        obias,
        gain_two,
        bias_two,
        up_grad,
        ubias,
        down_grad,
        dbias,
    )


def solution(mesh):
    return jax.shard_map(
        body,
        mesh=mesh,
        in_specs=(
            P("page", "strip", None, None),
            P("page", "strip", None),
            P("page", None, None),
            P("page", None),
            P("page"),
            P(),
            P(),
            P(),
            P(),
            P(),
            P(),
            P(),
            P(),
            P(),
            P(),
            P(),
            P("page", "strip", None, None),
            P("page", "strip", None),
        ),
        out_specs=(
            P("page", "strip", None, None),
            P("page", "strip", None),
            P("page", "strip", None, None),
            P("page", "strip", None),
            P(None, "strip"),
            P(None, "strip"),
            P(None, "strip", None),
            P(None, "strip", None),
            P(None, "strip"),
            P(None, "strip"),
            P(None, "strip"),
            P(None, "strip", None),
            P(None, "strip"),
            P(None, "strip", None),
            P(None, "strip"),
        ),
        check_vma=False,
    )
```

time: 1670 us -> 740 us (0.44)
  waiting for transfers between devices: 802 us -> 175 us
  matrix products: 291 us -> 30.8 us
  local copies, waits for them, and re-layouts: 341 us -> 111 us
  Pallas kernels: 0 us -> 188 us
  starting transfers between devices: 6.44 us -> 88 us
  other arithmetic: 117 us -> 43.4 us
    reduce_scatter x8 -> x0, waiting for transfers between devices: 471 us -> none  [the longest x1 189 us: body(): lax.psum_scatter(up_grad, 'strip', scatter_dimension=1, tiled=True)]
    dot_general x48 -> x10, matrix products: 291 us -> 30.8 us  [dot_tn(): lax.dot_general(a, b, (((0,), (0,)), ((), ())), preferred_element_type=f32)]
    pallas_call x0 -> x11, Pallas kernels: none -> 188 us  [the longest x1 45.6 us: attention_backward(): pl.pallas_call(functools.partial(attention_backward_kernel, windows), gri...]
    unnamed x26 -> x1, waiting for transfers between devices: 179 us -> 0.02 us
    ppermute x4 -> x62, waiting for transfers between devices: 10 us -> 175 us  [the longest x57 175 us: moved(): lax.ppermute(block, axis, [(i, (i + step) % size) for i in range(size)])]
    psum x1 -> x0, waiting for transfers between devices: 143 us -> none  [body(): lax.psum((gain_one, bias_one, qkv_grad, out_grad, obias_grad, gain_two, b...]
    reshape x42 -> x15, local copies, waits for them, and re-layouts: 136 us -> 27 us  [the longest x2 6.08 us: to_windows(): return rolled.reshape(WIN, across, WIN, rows.shape[-1]).transpose(1, 0, 2...]
    ppermute x4 -> x62, starting transfers between devices: 5.44 us -> 87.9 us  [the longest x57 87.1 us: moved(): lax.ppermute(block, axis, [(i, (i + step) % size) for i in range(size)])]
  transfers between devices with their start and end apart: 22 -> 63, of which waited for: 12 -> 27; matrix products, arithmetic and copies ran while one was open for 32% -> 24% of each run, Pallas kernels for 0% -> 26%
where the time goes in v1:
time: 740 us; the launch traced here: 732 us
  Pallas kernels  188 us (25%)
  waiting for transfers between devices  175 us (24%)
  local copies, waits for them, and re-layouts  111 us (15%)
  starting transfers between devices  88 us (12%)
  blocking collectives  79.8 us (11%)
  other arithmetic  43.4 us (6%)
  matrix products  30.8 us (4%)
  between operations  16.4 us (2%)
    ppermute x57, waiting for transfers between devices, moved(): lax.ppermute(block, axis, [(i, (i + step) % size) for i in range(size)])  175 us
    ppermute x57, starting transfers between devices, moved(): lax.ppermute(block, axis, [(i, (i + step) % size) for i in range(size)])  87.1 us
    pallas_call x1, Pallas kernels, attention_backward(): pl.pallas_call(functools.partial(attention_backward_kernel, windows), gri...  45.6 us
    pallas_call x2, Pallas kernels, ffn_forward(): pl.pallas_call(functools.partial(ffn_forward_kernel, stream), grid=(hidde...  42.5 us
    pallas_call x2, Pallas kernels, ffn_backward(): pl.pallas_call(functools.partial(ffn_backward_kernel, stream), grid=(hidd...  39.4 us
    psum x1, blocking collectives, body(): small = lax.psum(small, ('page', 'strip'))  38.6 us
    dot_general x10, matrix products, dot_tn(): lax.dot_general(a, b, (((0,), (0,)), ((), ())), preferred_element_type=f32)  30.8 us
    all_gather x1, blocking collectives, body(): query_cot = lax.all_gather(query_cotangent[0], 'strip', axis=0, tiled=True)  25.7 us
  transfers between devices with their start and end apart: 63, of which 27 were waited for; matrix products, arithmetic and copies ran while one was open for 24% of the time, Pallas kernels for 26%

profile of v1, /device:TPU:0, one launch (start us, length us, event | category | flops | bytes accessed | tf_op | source)
XLA Modules:
  0.0 731.9 jit_solution(17429234030491014877)
XLA Ops:
  9.7 4.5 collective-permute-start
  18.8 25.7 %all-gather.1 = bf16[1,256,768]{2,1,0:T(8,128)(2,1)} all-gather(bf16[1,32,768]{2,1,0:T(8,128)(2,1)S(1)} %copy-done.41), channel_id=3, replica_groups=mesh['page'=4,'strip'=8] {'strip'}, dimensions={1}, use_global_device_ids=true | all-gather | bytes 442368 | tf_op jit(solution)/shard_map/all_gather | solution.py:807
  44.5 15.5 %all-gather = bf16[1,256,768]{2,1,0:T(8,128)(2,1)} all-gather(bf16[1,32,768]{2,1,0:T(8,128)(2,1)S(1)} %copy-done.33), channel_id=2, replica_groups=mesh['page'=4,'strip'=8] {'strip'}, dimensions={1}, use_global_device_ids=true | all-gather | bytes 442368 | tf_op jit(solution)/shard_map/all_gather | solution.py:806
  61.6 4.9 norm_qkv.3
  78.6 9.9 %norm_qkv.2 = (bf16[1008,768]{1,0:T(8,128)(2,1)}, bf16[1008,2304]{1,0:T(8,128)(2,1)}) custom-call(bf16[1008,768]{1,0:T(8,128)(2,1)} %reshape.577.x_ref, f32[2,768]{1,0:T(2,128)} %gain_ref.15, f32[2,768]{1,0:T(2,128)} %bias_ref.5, bf16[2,768,2304]{2,1,0:T(8,128)(2,1)} %w_ref.7), custom_call_target="tpu_custom_call" | custom-call | flops 3567255552 | bytes 11280384 | tf_op jit(solution)/shard_map/norm_qkv/pallas_call | solution.py:90
  88.5 10.3 %query_forward.1 = (bf16[256,768]{1,0:T(8,128)(2,1)}, f32[6,1,512]{2,1,0:T(1,128)}) custom-call(bf16[256,2304]{1,0:T(8,128)(2,1)} %get-tuple-element.58.kq_ref.vq_ref.qq_ref, bf16[1008,2304]{1,0:T(8,128)(2,1)} %get-tuple-element.57.q_ref.k_ref.v_ref, bf16[1008,2304]{1,0:T(8,128)(2,1)} %get-tuple-element.57.q_ref.k_ref.v_ref, ...), custom_call_target="tpu_custom_call" | custom-call | flops 1635778560 | bytes 3096576 | tf_op jit(solution)/shard_map/query_forward/pallas_call | solution.py:162
  105.2 20.2 %window_forward.1 = (bf16[1008,768]{1,0:T(8,128)(2,1)}, f32[6,7,288]{2,1,0:T(8,128)}) custom-call(bf16[1008,2304]{1,0:T(8,128)(2,1)} %get-tuple-element.57.q_ref.k_ref.v_ref, bf16[1008,2304]{1,0:T(8,128)(2,1)} %get-tuple-element.57.q_ref.k_ref.v_ref, bf16[1008,2304]{1,0:T(8,128)(2,1)} %get-tuple-element.57.q_ref.k_ref.v_ref, ...), custom_call_target="tpu_custom_call" | custom-call | flops 2477260800 | bytes 6193152 | tf_op jit(solution)/shard_map/window_forward/pallas_call | solution.py:218
  125.4 30.9 %ffn_forward.2 = (f32[1008,768]{1,0:T(8,128)}, bf16[1008,768]{1,0:T(8,128)(2,1)}, bf16[1008,3072]{1,0:T(8,128)(2,1)}, bf16[1008,3072]{1,0:T(8,128)(2,1)}, bf16[1008,768]{1,0:T(8,128)(2,1)}) custom-call(bf16[1008,768]{1,0:T(8,128)(2,1)} %reshape.577.x_ref, bf16[1008,768]{1,0:T(8,128)(2,1)} %get-tuple-element.59.o_ref, bf16[2,768,768]{2,1,0:T(8,128)(2,1)} %wo_ref.7, ...), custom_call_target="tpu_custom_call" | custom-call | flops 10701766656 | bytes 31113216 | tf_op jit(solution)/shard_map/ffn_forward/pallas_call | solution.py:486
  179.0 8.5 %convolution_convert_fusion = bf16[3072,768]{1,0:T(8,128)(2,1)S(1)} fusion(bf16[1008,3072]{1,0:T(8,128)(2,1)} %get-tuple-element.97, bf16[1008,768]{1,0:T(8,128)(2,1)S(1)} %reshape.583.g_ref), kind=kOutput, calls=%fused_computation.6 | convolution fusion | flops 4758700032 | bytes 12460032 | tf_op jit(solution)/shard_map/dot_general | solution.py:42
  187.5 28.2 %ffn_backward.2 = (bf16[1008,3072]{1,0:T(8,128)(2,1)}, f32[1,3072]{1,0:T(1,128)}, f32[1008,768]{1,0:T(8,128)}, bf16[1008,768]{1,0:T(8,128)(2,1)}, bf16[1008,768]{1,0:T(8,128)(2,1)}, /*index=5*/f32[8,768]{1,0:T(8,128)}) custom-call(bf16[1008,768]{1,0:T(8,128)(2,1)} %copy-done.19, bf16[1008,3072]{1,0:T(8,128)(2,1)} %get-tuple-element.64.slope_ref, ...), custom_call_target="tpu_custom_call" | custom-call | flops 10701766656 | bytes 32661504 | tf_op jit(solution)/shard_map/ffn_backward/pallas_call | solution.py:588
  222.3 5.4 convolution_convert_fusion.1
  236.9 4.2 collective-permute-done.10
  261.8 39.5 %collective-permute-done.4 = bf16[256,768]{1,0:T(8,128)(2,1)S(1)} collective-permute-done((bf16[256,768]{1,0:T(8,128)(2,1)}, bf16[256,768]{1,0:T(8,128)(2,1)S(1)}, u32[]{:S(2)}, u32[]{:S(2)}) %collective-permute-start.4) | collective-permute-done | bytes 393248 | tf_op jit(solution)/shard_map/ppermute | solution.py:671
  325.6 11.6 %ffn_forward.3 = (f32[256,768]{1,0:T(8,128)}, bf16[256,768]{1,0:T(8,128)(2,1)}, bf16[256,3072]{1,0:T(8,128)(2,1)}, bf16[256,3072]{1,0:T(8,128)(2,1)}, bf16[256,768]{1,0:T(8,128)(2,1)}) custom-call(bf16[256,768]{1,0:T(8,128)(2,1)} %bitcast.346, bf16[256,768]{1,0:T(8,128)(2,1)} %convert_element_type.286.o_ref, bf16[2,768,768]{2,1,0:T(8,128)(2,1)} %wo_ref.7, ...), custom_call_target="tpu_custom_call" | custom-call | flops 2717908992 | bytes 14942208 | tf_op jit(solution)/shard_map/ffn_forward/pallas_call | solution.py:486
  337.2 11.2 %ffn_backward.3 = (bf16[256,3072]{1,0:T(8,128)(2,1)}, f32[1,3072]{1,0:T(1,128)}, f32[256,768]{1,0:T(8,128)}, bf16[256,768]{1,0:T(8,128)(2,1)}, bf16[256,768]{1,0:T(8,128)(2,1)}, /*index=5*/f32[8,768]{1,0:T(8,128)}) custom-call(bf16[256,768]{1,0:T(8,128)(2,1)} %bitcast.347, bf16[256,3072]{1,0:T(8,128)(2,1)} %get-tuple-element.67.slope_ref, ...), custom_call_target="tpu_custom_call" | custom-call | flops 2717908992 | bytes 15335424 | tf_op jit(solution)/shard_map/ffn_backward/pallas_call | solution.py:588
  350.4 45.6 %attention_backward.1 = (bf16[1008,768]{1,0:T(8,128)(2,1)}, bf16[1008,768]{1,0:T(8,128)(2,1)}, bf16[1008,768]{1,0:T(8,128)(2,1)}, f32[256,768]{1,0:T(8,128)}, f3...) custom-call(bf16[1008,2304]{1,0:T(8,128)(2,1)} %get-tuple-element.57.q_ref.k_ref.v_ref, ...), custom_call_target="tpu_custom_call" | custom-call | flops 10156769280 | bytes 10838016 | tf_op jit(solution)/shard_map/attention_backward/pallas_call | solution.py:365
  396.0 11.2 %input_grad.2 = (bf16[1008,768]{1,0:T(8,128)(2,1)}, f32[8,768]{1,0:T(8,128)}) custom-call(bf16[1008,768]{1,0:T(8,128)(2,1)} %get-tuple-element.71.dq_ref, bf16[1008,768]{1,0:T(8,128)(2,1)} %get-tuple-element.72.dk_ref, bf16[1008,768]{1,0:T(8,128)(2,1)} %get-tuple-element.73.dv_ref, bf16[2,768,2304]{2,1,0:T(8,128)(2,1)} %w_ref.7, ...), custom_call_target="tpu_custom_call" | custom-call | flops 3567255552 | bytes 14376960 | tf_op jit(solution)/shard_map/input_grad/pallas_call | solution.py:648
  425.8 4.3 copy.135
  454.2 6.2 collective-permute-done.34
  487.1 14.2 %collective-permute-done.20 = bf16[32,2304]{1,0:T(8,128)(2,1)S(1)} collective-permute-done((bf16[32,2304]{1,0:T(8,128)(2,1)S(1)}, bf16[32,2304]{1,0:T(8,128)(2,1)S(1)}, u32[]{:S(2)}, u32[]{:S(2)}) %collective-permute-start.20) | collective-permute-done | bytes 147488 | tf_op jit(solution)/shard_map/ppermute | solution.py:671
  503.6 4.1 input_grad.3
  508.5 38.6 %psum.7 = f32[2,10,768]{2,1,0:T(8,128)} all-reduce(f32[2,10,768]{2,1,0:T(8,128)S(1)} %pad_maximum_fusion.8), channel_id=1, replica_groups=mesh['page'=4,'strip'=8] {'page','strip'}, use_global_device_ids=true, to_apply=%region_3.4 | all-reduce | flops 15360 | bytes 122880 | tf_op jit(solution)/shard_map/psum | solution.py:929
  571.6 6.2 collective-permute-done.53
  581.7 7.3 collective-permute-done.55
  589.0 24.6 %collective-permute-done.54 = bf16[384,768]{1,0:T(8,128)(2,1)S(1)} collective-permute-done((bf16[384,768]{1,0:T(8,128)(2,1)S(1)}, bf16[384,768]{1,0:T(8,128)(2,1)S(1)}, u32[]{:S(2)}, u32[]{:S(2)}) %collective-permute-start.54) | collective-permute-done | bytes 589856 | tf_op jit(solution)/shard_map/ppermute | solution.py:671
  619.8 3.8 collective-permute-start.48
  642.8 14.2 %collective-permute-done.49 = bf16[2,24,3072]{2,1,0:T(8,128)(2,1)S(1)} collective-permute-done((bf16[2,24,3072]{2,1,0:T(8,128)(2,1)S(1)}, bf16[2,24,3072]{2,1,0:T(8,128)(2,1)S(1)}, u32[]{:S(2)}, u32[]{:S(2)}) %collective-permute-start.49) | collective-permute-done | bytes 294944 | tf_op jit(solution)/shard_map/ppermute | solution.py:671
  658.6 7.1 collective-permute-done.50
  665.7 13.8 %collective-permute-start.59 = (bf16[2,96,768]{2,1,0:T(8,128)(2,1)S(1)}, bf16[2,96,768]{2,1,0:T(8,128)(2,1)S(1)}, u32[]{:S(2)}, u32[]{:S(2)}) collective-permute-start(bf16[2,96,768]{2,1,0:T(8,128)(2,1)S(1)} %get-tuple-element.100), channel_id=1, source_target_pairs={{0,24},{8,0},{16,8},{24,16},{1,25},{9,1},{17,9},{25,17},{2,26},{10... | collective-permute-start | bytes 884744 | tf_op jit(solution)/shard_map/ppermute | solution.py:671
  679.5 6.5 collective-permute-done.59
  689.2 6.4 collective-permute-done.61
  714.7 5.9 collective-permute-done.29
  (424 shorter events, 265.1 us)
Async XLA Ops:
  7.2 616.4 %all-gather.4.cloned.1.call-start = ((), (), s32[]{:S(2)}) async-start(), calls=%async_computation | async-start | bytes 1327104 | tf_op jit(solution)/shard_map/all_gather | solution.py:895
  9.7 59.7 %collective-permute-start = (bf16[6,84,768]{2,1,0:T(8,128)(2,1)}, bf16[6,84,768]{2,1,0:T(8,128)(2,1)S(1)}, u32[]{:S(2)}, u32[]{:S(2)}) collective-permute-start(bf16[6,84,768]{2,1,0:T(8,128)(2,1)} %get-tuple-element.117), channel_id=1, source_target_pairs={{0,7},{1,0},{2,1},{3,2},{4,3},{5,4},{6,5},{7,6},{8,15},{9,8},{10,9... | collective-permute-start | bytes 2322440 | tf_op jit(solution)/shard_map/ppermute | solution.py:671
  15.3 151.2 %collective-permute-start.16 = (bf16[6,84,768]{2,1,0:T(8,128)(2,1)}, bf16[6,84,768]{2,1,0:T(8,128)(2,1)}, u32[]{:S(2)}, u32[]{:S(2)}) collective-permute-start(bf16[6,84,768]{2,1,0:T(8,128)(2,1)} %get-tuple-element.115), channel_id=1, source_target_pairs={{0,7},{1,0},{2,1},{3,2},{4,3},{5,4},{6,5},{7,6},{8,15},{9,8},{10,9... | collective-permute-start | bytes 2322440 | tf_op jit(solution)/shard_map/ppermute | solution.py:671
  98.8 151.3 %collective-permute-start.15 = (f32[6,1,512]{2,1,0:T(1,128)}, f32[6,1,512]{2,1,0:T(1,128)}, u32[]{:S(2)}, u32[]{:S(2)}) collective-permute-start(f32[6,1,512]{2,1,0:T(1,128)} %get-tuple-element.62), channel_id=1, source_target_pairs={{0,7},{1,0},{2,1},{3,2},{4,3},{5,4},{6,5},{7,6},{8,15},{9,8},{10,9... | collective-permute-start | bytes 36872 | tf_op jit(solution)/shard_map/ppermute | solution.py:671
  102.2 150.0 %collective-permute-start.14 = (f32[6,1,512]{2,1,0:T(1,128)}, f32[6,1,512]{2,1,0:T(1,128)}, u32[]{:S(2)}, u32[]{:S(2)}) collective-permute-start(f32[6,1,512]{2,1,0:T(1,128)} %get-tuple-element.62), channel_id=1, source_target_pairs={{0,6},{1,7},{2,0},{3,1},{4,2},{5,3},{6,4},{7,5},{8,14},{9,15},{10,... | collective-permute-start | bytes 36872 | tf_op jit(solution)/shard_map/ppermute | solution.py:671
  102.3 145.0 %collective-permute-start.13 = (f32[6,1,512]{2,1,0:T(1,128)}, f32[6,1,512]{2,1,0:T(1,128)}, u32[]{:S(2)}, u32[]{:S(2)}) collective-permute-start(f32[6,1,512]{2,1,0:T(1,128)} %get-tuple-element.62), channel_id=1, source_target_pairs={{0,5},{1,6},{2,7},{3,0},{4,1},{5,2},{6,3},{7,4},{8,13},{9,14},{10,... | collective-permute-start | bytes 36872 | tf_op jit(solution)/shard_map/ppermute | solution.py:671
  102.5 143.2 %collective-permute-start.12 = (f32[6,1,512]{2,1,0:T(1,128)}, f32[6,1,512]{2,1,0:T(1,128)}, u32[]{:S(2)}, u32[]{:S(2)}) collective-permute-start(f32[6,1,512]{2,1,0:T(1,128)} %get-tuple-element.62), channel_id=1, source_target_pairs={{0,4},{1,5},{2,6},{3,7},{4,0},{5,1},{6,2},{7,3},{8,12},{9,13},{10,... | collective-permute-start | bytes 36872 | tf_op jit(solution)/shard_map/ppermute | solution.py:671
  166.5 69.0 %collective-permute-start.9 = (f32[6,1,512]{2,1,0:T(1,128)S(1)}, f32[6,1,512]{2,1,0:T(1,128)}, u32[]{:S(2)}, u32[]{:S(2)}) collective-permute-start(f32[6,1,512]{2,1,0:T(1,128)S(1)} %copy-done.34), channel_id=1, source_target_pairs={{0,1},{1,2},{2,3},{3,4},{4,5},{5,6},{6,7},{7,0},{8,9},{9,10},{10,1... | collective-permute-start | bytes 36872 | tf_op jit(solution)/shard_map/ppermute | solution.py:671
  245.1 65.9 %collective-permute-start.7 = (bf16[256,768]{1,0:T(8,128)(2,1)}, bf16[256,768]{1,0:T(8,128)(2,1)}, u32[]{:S(2)}, u32[]{:S(2)}) collective-permute-start(bf16[256,768]{1,0:T(8,128)(2,1)} %get-tuple-element.61), channel_id=1, source_target_pairs={{0,6},{1,7},{2,0},{3,1},{4,2},{5,3},{6,4},{7,5},{8,14},{9,15},{10,... | collective-permute-start | bytes 1179656 | tf_op jit(solution)/shard_map/ppermute | solution.py:671
  245.8 67.2 %collective-permute-start.6 = (bf16[256,768]{1,0:T(8,128)(2,1)}, bf16[256,768]{1,0:T(8,128)(2,1)}, u32[]{:S(2)}, u32[]{:S(2)}) collective-permute-start(bf16[256,768]{1,0:T(8,128)(2,1)} %get-tuple-element.61), channel_id=1, source_target_pairs={{0,5},{1,6},{2,7},{3,0},{4,1},{5,2},{6,3},{7,4},{8,13},{9,14},{10,... | collective-permute-start | bytes 1179656 | tf_op jit(solution)/shard_map/ppermute | solution.py:671
  247.3 54.0 %collective-permute-start.4 = (bf16[256,768]{1,0:T(8,128)(2,1)}, bf16[256,768]{1,0:T(8,128)(2,1)S(1)}, u32[]{:S(2)}, u32[]{:S(2)}) collective-permute-start(bf16[256,768]{1,0:T(8,128)(2,1)} %get-tuple-element.61), channel_id=1, source_target_pairs={{0,3},{1,4},{2,5},{3,6},{4,7},{5,0},{6,1},{7,2},{8,11},{9,12},{10,... | collective-permute-start | bytes 1179656 | tf_op jit(solution)/shard_map/ppermute | solution.py:671
  250.1 54.4 %collective-permute-start.3 = (bf16[256,768]{1,0:T(8,128)(2,1)}, bf16[256,768]{1,0:T(8,128)(2,1)}, u32[]{:S(2)}, u32[]{:S(2)}) collective-permute-start(bf16[256,768]{1,0:T(8,128)(2,1)} %get-tuple-element.61), channel_id=1, source_target_pairs={{0,2},{1,3},{2,4},{3,5},{4,6},{5,7},{6,0},{7,1},{8,10},{9,11},{10,... | collective-permute-start | bytes 1179656 | tf_op jit(solution)/shard_map/ppermute | solution.py:671
  252.1 54.4 %collective-permute-start.2 = (bf16[256,768]{1,0:T(8,128)(2,1)}, bf16[256,768]{1,0:T(8,128)(2,1)}, u32[]{:S(2)}, u32[]{:S(2)}) collective-permute-start(bf16[256,768]{1,0:T(8,128)(2,1)} %get-tuple-element.61), channel_id=1, source_target_pairs={{0,1},{1,2},{2,3},{3,4},{4,5},{5,6},{6,7},{7,0},{8,9},{9,10},{10,1... | collective-permute-start | bytes 1179656 | tf_op jit(solution)/shard_map/ppermute | solution.py:671
  306.5 163.9 %collective-permute-start.1 = (bf16[6,84,768]{2,1,0:T(8,128)(2,1)}, bf16[6,84,768]{2,1,0:T(8,128)(2,1)}, u32[]{:S(2)}, u32[]{:S(2)}) collective-permute-start(bf16[6,84,768]{2,1,0:T(8,128)(2,1)} %fusion.23), channel_id=1, source_target_pairs={{0,1},{1,2},{2,3},{3,4},{4,5},{5,6},{6,7},{7,0},{8,9},{9,10},{10,1... | collective-permute-start | bytes 2322440 | tf_op jit(solution)/shard_map/ppermute | solution.py:671
  311.0 128.8 %collective-permute-start.32 = (bf16[4,96,768]{2,1,0:T(8,128)(2,1)}, bf16[4,96,768]{2,1,0:T(8,128)(2,1)}, u32[]{:S(2)}, u32[]{:S(2)}) collective-permute-start(bf16[4,96,768]{2,1,0:T(8,128)(2,1)} %dynamic-slice_bitcast_fusion.6), channel_id=1, source_target_pairs={{0,1},{1,0},{2,3},{3,2},{4,5},{5,4},{6,7},{7,6},{8,9},{9,8},{10,11... | collective-permute-start | bytes 1769480 | tf_op jit(solution)/shard_map/ppermute | solution.py:676
  312.9 243.3 %collective-permute-start.52 = (bf16[4,384,768]{2,1,0:T(8,128)(2,1)}, bf16[4,384,768]{2,1,0:T(8,128)(2,1)}, u32[]{:S(2)}, u32[]{:S(2)}) collective-permute-start(bf16[4,384,768]{2,1,0:T(8,128)(2,1)} %dynamic-slice_bitcast_fusion), channel_id=1, source_target_pairs={{0,1},{1,0},{2,3},{3,2},{4,5},{5,4},{6,7},{7,6},{8,9},{9,8},{10,11... | collective-permute-start | bytes 7077896 | tf_op jit(solution)/shard_map/ppermute | solution.py:676
  466.5 98.2 %collective-permute-start.42 = (bf16[4,96,3072]{2,1,0:T(8,128)(2,1)}, bf16[4,96,3072]{2,1,0:T(8,128)(2,1)}, u32[]{:S(2)}, u32[]{:S(2)}) collective-permute-start(bf16[4,96,3072]{2,1,0:T(8,128)(2,1)} %dynamic-slice_bitcast_fusion.1), channel_id=1, source_target_pairs={{0,1},{1,0},{2,3},{3,2},{4,5},{5,4},{6,7},{7,6},{8,9},{9,8},{10,11... | collective-permute-start | bytes 7077896 | tf_op jit(solution)/shard_map/ppermute | solution.py:676
  487.1 66.5 %collective-permute-start.17 = (bf16[6,84,768]{2,1,0:T(8,128)(2,1)}, bf16[6,84,768]{2,1,0:T(8,128)(2,1)}, u32[]{:S(2)}, u32[]{:S(2)}) collective-permute-start(bf16[6,84,768]{2,1,0:T(8,128)(2,1)} %fusion.22), channel_id=1, source_target_pairs={{0,1},{1,2},{2,3},{3,4},{4,5},{5,6},{6,7},{7,0},{8,9},{9,10},{10,1... | collective-permute-start | bytes 2322440 | tf_op jit(solution)/shard_map/ppermute | solution.py:671
  487.1 82.8 %collective-permute-start.22 = (bf16[4,96,2304]{2,1,0:T(8,128)(2,1)}, bf16[4,96,2304]{2,1,0:T(8,128)(2,1)S(1)}, u32[]{:S(2)}, u32[]{:S(2)}) collective-permute-start(bf16[4,96,2304]{2,1,0:T(8,128)(2,1)} %dynamic-slice_bitcast_fusion.2), channel_id=1, source_target_pairs={{0,1},{1,0},{2,3},{3,2},{4,5},{5,4},{6,7},{7,6},{8,9},{9,8},{10,11... | collective-permute-start | bytes 5308424 | tf_op jit(solution)/shard_map/ppermute | solution.py:676
  562.5 26.5 %collective-permute-start.55 = (bf16[384,768]{1,0:T(8,128)(2,1)S(1)}, bf16[384,768]{1,0:T(8,128)(2,1)S(1)}, u32[]{:S(2)}, u32[]{:S(2)}) collective-permute-start(bf16[384,768]{1,0:T(8,128)(2,1)S(1)} %get-tuple-element.109), channel_id=1, source_target_pairs={{0,6},{1,7},{2,0},{3,1},{4,2},{5,3},{6,4},{7,5},{8,14},{9,15},{10,... | collective-permute-start | bytes 1769480 | tf_op jit(solution)/shard_map/ppermute | solution.py:671
  563.5 50.2 %collective-permute-start.54 = (bf16[384,768]{1,0:T(8,128)(2,1)S(1)}, bf16[384,768]{1,0:T(8,128)(2,1)S(1)}, u32[]{:S(2)}, u32[]{:S(2)}) collective-permute-start(bf16[384,768]{1,0:T(8,128)(2,1)S(1)} %get-tuple-element.110), channel_id=1, source_target_pairs={{0,4},{1,5},{2,6},{3,7},{4,0},{5,1},{6,2},{7,3},{8,12},{9,13},{10,... | collective-permute-start | bytes 1769480 | tf_op jit(solution)/shard_map/ppermute | solution.py:671
  567.5 50.3 %collective-permute-start.43 = (bf16[5,24,3072]{2,1,0:T(8,128)(2,1)S(1)}, bf16[5,24,3072]{2,1,0:T(8,128)(2,1)S(1)}, u32[]{:S(2)}, u32[]{:S(2)}) collective-permute-start(bf16[5,24,3072]{2,1,0:T(8,128)(2,1)S(1)} %get-tuple-element.105), channel_id=1, source_target_pairs={{0,8},{8,16},{16,24},{24,0},{1,9},{9,17},{17,25},{25,1},{2,10},{10... | collective-permute-start | bytes 2211848 | tf_op jit(solution)/shard_map/ppermute | solution.py:671
  569.8 48.0 %collective-permute-start.44 = (bf16[5,24,3072]{2,1,0:T(8,128)(2,1)S(1)}, bf16[5,24,3072]{2,1,0:T(8,128)(2,1)S(1)}, u32[]{:S(2)}, u32[]{:S(2)}) collective-permute-start(bf16[5,24,3072]{2,1,0:T(8,128)(2,1)S(1)} %get-tuple-element.106), channel_id=1, source_target_pairs={{0,16},{8,24},{16,0},{24,8},{1,17},{9,25},{17,1},{25,9},{2,18},{10... | collective-permute-start | bytes 2211848 | tf_op jit(solution)/shard_map/ppermute | solution.py:671
  577.8 40.0 %collective-permute-start.45 = (bf16[5,24,3072]{2,1,0:T(8,128)(2,1)S(1)}, bf16[5,24,3072]{2,1,0:T(8,128)(2,1)S(1)}, u32[]{:S(2)}, u32[]{:S(2)}) collective-permute-start(bf16[5,24,3072]{2,1,0:T(8,128)(2,1)S(1)} %get-tuple-element.107), channel_id=1, source_target_pairs={{0,24},{8,0},{16,8},{24,16},{1,25},{9,1},{17,9},{25,17},{2,26},{10... | collective-permute-start | bytes 2211848 | tf_op jit(solution)/shard_map/ppermute | solution.py:671
  614.9 24.0 %collective-permute-start.56 = (bf16[2,96,768]{2,1,0:T(8,128)(2,1)}, bf16[2,96,768]{2,1,0:T(8,128)(2,1)}, u32[]{:S(2)}, u32[]{:S(2)}) collective-permute-start(bf16[2,96,768]{2,1,0:T(8,128)(2,1)} %get-tuple-element.118), channel_id=1, source_target_pairs={{0,8},{8,16},{16,24},{24,0},{1,9},{9,17},{17,25},{25,1},{2,10},{10... | collective-permute-start | bytes 884744 | tf_op jit(solution)/shard_map/ppermute | solution.py:671
  617.5 21.8 %collective-permute-start.57 = (bf16[2,96,768]{2,1,0:T(8,128)(2,1)}, bf16[2,96,768]{2,1,0:T(8,128)(2,1)}, u32[]{:S(2)}, u32[]{:S(2)}) collective-permute-start(bf16[2,96,768]{2,1,0:T(8,128)(2,1)} %get-tuple-element.119), channel_id=1, source_target_pairs={{0,16},{8,24},{16,0},{24,8},{1,17},{9,25},{17,1},{25,9},{2,18},{10... | collective-permute-start | bytes 884744 | tf_op jit(solution)/shard_map/ppermute | solution.py:671
  631.3 69.3 %collective-permute-start.23 = (bf16[5,24,2304]{2,1,0:T(8,128)(2,1)S(1)}, bf16[5,24,2304]{2,1,0:T(8,128)(2,1)S(1)}, u32[]{:S(2)}, u32[]{:S(2)}) collective-permute-start(bf16[5,24,2304]{2,1,0:T(8,128)(2,1)S(1)} %get-tuple-element.111), channel_id=1, source_target_pairs={{0,8},{8,16},{16,24},{24,0},{1,9},{9,17},{17,25},{25,1},{2,10},{10... | collective-permute-start | bytes 1658888 | tf_op jit(solution)/shard_map/ppermute | solution.py:671
  636.2 20.8 %collective-permute-start.49 = (bf16[2,24,3072]{2,1,0:T(8,128)(2,1)S(1)}, bf16[2,24,3072]{2,1,0:T(8,128)(2,1)S(1)}, u32[]{:S(2)}, u32[]{:S(2)}) collective-permute-start(bf16[2,24,3072]{2,1,0:T(8,128)(2,1)S(1)} %pad_maximum_fusion.6), channel_id=1, source_target_pairs={{0,24},{8,0},{16,8},{24,16},{1,25},{9,1},{17,9},{25,17},{2,26},{10... | collective-permute-start | bytes 884744 | tf_op jit(solution)/shard_map/ppermute | solution.py:671
  638.9 61.7 %collective-permute-start.24 = (bf16[5,24,2304]{2,1,0:T(8,128)(2,1)S(1)}, bf16[5,24,2304]{2,1,0:T(8,128)(2,1)S(1)}, u32[]{:S(2)}, u32[]{:S(2)}) collective-permute-start(bf16[5,24,2304]{2,1,0:T(8,128)(2,1)S(1)} %get-tuple-element.112), channel_id=1, source_target_pairs={{0,16},{8,24},{16,0},{24,8},{1,17},{9,25},{17,1},{25,9},{2,18},{10... | collective-permute-start | bytes 1658888 | tf_op jit(solution)/shard_map/ppermute | solution.py:671
  639.3 61.4 %collective-permute-start.25 = (bf16[5,24,2304]{2,1,0:T(8,128)(2,1)S(1)}, bf16[5,24,2304]{2,1,0:T(8,128)(2,1)S(1)}, u32[]{:S(2)}, u32[]{:S(2)}) collective-permute-start(bf16[5,24,2304]{2,1,0:T(8,128)(2,1)S(1)} %get-tuple-element.113), channel_id=1, source_target_pairs={{0,24},{8,0},{16,8},{24,16},{1,25},{9,1},{17,9},{25,17},{2,26},{10... | collective-permute-start | bytes 1658888 | tf_op jit(solution)/shard_map/ppermute | solution.py:671
  639.8 25.9 %collective-permute-start.50 = (bf16[2,24,3072]{2,1,0:T(8,128)(2,1)S(1)}, bf16[2,24,3072]{2,1,0:T(8,128)(2,1)S(1)}, u32[]{:S(2)}, u32[]{:S(2)}) collective-permute-start(bf16[2,24,3072]{2,1,0:T(8,128)(2,1)S(1)} %pad_maximum_fusion.6), channel_id=1, source_target_pairs={{0,16},{8,24},{16,0},{24,8},{1,17},{9,25},{17,1},{25,9},{2,18},{10... | collective-permute-start | bytes 884744 | tf_op jit(solution)/shard_map/ppermute | solution.py:671
  657.0 29.5 %collective-permute-start.60 = (bf16[2,96,768]{2,1,0:T(8,128)(2,1)S(1)}, bf16[2,96,768]{2,1,0:T(8,128)(2,1)S(1)}, u32[]{:S(2)}, u32[]{:S(2)}) collective-permute-start(bf16[2,96,768]{2,1,0:T(8,128)(2,1)S(1)} %get-tuple-element.100), channel_id=1, source_target_pairs={{0,16},{8,24},{16,0},{24,8},{1,17},{9,25},{17,1},{25,9},{2,18},{10... | collective-permute-start | bytes 884744 | tf_op jit(solution)/shard_map/ppermute | solution.py:671
  (86 other events, 957.2 us)
Sparse Core Ops, SparseCore 0:
  502.2 20.7 all-gather.3
